TPU v7x, 128 devices: a whole 4x4x4 slice. The times are simulated.
128 devices in a mesh: ha: 16 (over y_hi, x, core), wa: 8 (over y_lo, z).
Axes of the slice: x: 4, y: 4 (y_hi: 2, y_lo: 2; y = y_hi * 2 + y_lo), z: 4, core: 2. Of those that a mesh axis runs over, the one named last changes fastest.
Arguments:
- hw_plane: bfloat16 [512, 1024, 128], P('ha', 'wa'), may hold values from -200 to 200
- zh_plane: bfloat16 [64, 512, 128], P(None, 'ha'), may hold values from -5 to 5
- wz_plane: bfloat16 [1024, 64, 128], P('wa'), may hold values from -5 to 5
- w_in: bfloat16 [128, 256], replicated, may hold values from -0.5 to 0.5
- b_in: float32 [256], replicated, may hold values from -3 to 3
- w_out: bfloat16 [256, 18], replicated, may hold values from -0.75 to 0.75
- b_out: float32 [18], replicated, may hold values from -3 to 3
- run_index: int32 [128, 512], P(('ha', 'wa')), may hold values from 0 to 2047, as said below
- run_count: int32 [128], P(('ha', 'wa')), may hold values from 1 to 511, as said below
- labels: int32 [128, 512, 128], P(('ha', 'wa')), may hold values from 0 to 17
Outputs:
- hw_grad: float32 [512, 1024, 128], P('ha', 'wa')
- zh_grad: float32 [64, 512, 128], P('wa', 'ha')
- wz_grad: float32 [1024, 64, 128], P('wa', 'ha')
- w_in_grad: float32 [128, 256], replicated
- b_in_grad: float32 [256], replicated
- w_out_grad: float32 [256, 18], replicated
- b_out_grad: float32 [18], replicated
Inputs may be any that keep to these rules, and one draw needn't show every extreme that they name: `run_index`: each row holds 512 different run positions of one device block. `run_count`: the counts of block k and of block k + 16 * 8 / 2 (ha index differing by 8) sum to exactly 512.
All inputs are finite; a program needn't handle non-finite values.
Results may differ from a plain program's by a relative error of at most 0.00055.
The roundings to bfloat16 on the way count: a program that leaves them out, or rounds other values in their place, can miss the bound.
Values may be sent and summed in bfloat16 or wider, within the bound.
A program may use at most 192 MiB of HBM per device.

v0:
```python
import math

import jax
import jax.numpy as jnp
from jax import lax
from jax.sharding import PartitionSpec as P

grad_scale = 0.25


def silu_slope(preact):
    sigmoid_val = jax.nn.sigmoid(preact)
    return sigmoid_val * (1.0 + preact * (1.0 - sigmoid_val))


def contract_rows(left, right):
    return lax.dot_general(
        left, right, (((0,), (0,)), ((), ())), preferred_element_type=jnp.float32
    )


def contract_cols(left, right):
    return lax.dot_general(
        left, right, (((1,), (1,)), ((), ())), preferred_element_type=jnp.float32
    )


def sample_grads(features, labels_flat, validity, w_in, b_in, w_out, b_out):
    preact = jnp.dot(features, w_in, preferred_element_type=jnp.float32) + b_in
    hidden = jax.nn.silu(preact).astype(jnp.bfloat16)
    logits = jnp.dot(hidden, w_out, preferred_element_type=jnp.float32) + b_out
    row_top = jnp.max(logits, axis=1, keepdims=True)
    scores_exp = jnp.exp(logits - row_top)
    probability = scores_exp / jnp.sum(scores_exp, axis=1, keepdims=True)
    classes = jnp.arange(logits.shape[1], dtype=jnp.int32)
    onehot = (labels_flat[:, None] == classes[None, :]).astype(jnp.float32)
    dlogits = ((probability - onehot) * (grad_scale * validity[:, None])).astype(jnp.bfloat16)
    grad_w_out = contract_rows(hidden, dlogits)
    grad_b_out = jnp.sum(dlogits.astype(jnp.float32), axis=0)
    dhidden = contract_cols(dlogits, w_out)
    dpreact = (dhidden * silu_slope(preact)).astype(jnp.bfloat16)
    grad_w_in = contract_rows(features, dpreact)
    grad_b_in = jnp.sum(dpreact.astype(jnp.float32), axis=0)
    dfeatures = contract_cols(dpreact, w_in)
    return (dfeatures, (grad_w_in, grad_b_in, grad_w_out, grad_b_out))


def run_features(hw_block, zh_rows, wz_block, run_ids):
    rows_blk, cols_blk, channels = hw_block.shape
    pair_cols = cols_blk // 2
    depth_z = wz_block.shape[1]
    run_row = run_ids // pair_cols
    run_pair = run_ids % pair_cols
    hw_part = hw_block.reshape(rows_blk * pair_cols, 2, channels)[run_ids].astype(jnp.float32)
    zh_part = zh_rows[run_row].astype(jnp.float32)
    wz_part = wz_block.reshape(pair_cols, 2, depth_z, channels)[run_pair].astype(jnp.float32)
    summed = hw_part[:, :, None, :] + zh_part[:, None, :, :] + wz_part
    return summed.astype(jnp.bfloat16)


def plane_grads(dfeatures, run_ids, rows_blk, cols_blk):
    slot_count, pair_count, depth_z, channels = dfeatures.shape
    pair_cols = cols_blk // 2
    run_row = run_ids // pair_cols
    run_pair = run_ids % pair_cols
    hw_local = jnp.zeros((rows_blk * pair_cols, 2, channels), jnp.float32)
    hw_local = (
        hw_local.at[run_ids].add(jnp.sum(dfeatures, axis=2)).reshape(rows_blk, cols_blk, channels)
    )
    zh_rows_grad = (
        jnp.zeros((rows_blk, depth_z, channels), jnp.float32)
        .at[run_row]
        .add(jnp.sum(dfeatures, axis=1))
    )
    zh_local = jnp.transpose(zh_rows_grad, (1, 0, 2))
    wz_local = jnp.zeros((pair_cols, 2, depth_z, channels), jnp.float32).at[run_pair].add(dfeatures)
    return (hw_local, zh_local, wz_local.reshape(cols_blk, depth_z, channels))


def decode(features, run_labels, validity, w_in, b_in, w_out, b_out):
    slot_count, pair_count, depth_z, channels = features.shape
    block_runs = math.gcd(32, slot_count)
    blocks = slot_count // block_runs
    block_rows = block_runs * pair_count * depth_z
    feat_blocks = features.reshape(blocks, block_rows, channels)
    label_blocks = run_labels.reshape(blocks, block_rows)
    valid_blocks = jnp.repeat(validity, pair_count * depth_z).reshape(blocks, block_rows)
    zero_init = (
        jnp.zeros(w_in.shape, jnp.float32),
        jnp.zeros(b_in.shape, jnp.float32),
        jnp.zeros(w_out.shape, jnp.float32),
        jnp.zeros(b_out.shape, jnp.float32),
    )

    def block_step(totals, pieces):
        dfeat, grads = sample_grads(pieces[0], pieces[1], pieces[2], w_in, b_in, w_out, b_out)
        return (jax.tree.map(jnp.add, totals, grads), dfeat)

    totals, dfeat_blocks = lax.scan(
        block_step, zero_init, (feat_blocks, label_blocks, valid_blocks)
    )
    return (dfeat_blocks.reshape(slot_count, pair_count, depth_z, channels), totals)


def local(hw_plane, zh_plane, wz_plane, w_in, b_in, w_out, b_out, run_index, run_count, labels):
    rows_blk, cols_blk, channels = hw_plane.shape
    capacity = run_index.shape[1]
    run_ids = run_index[0]
    run_total = run_count[0]
    run_labels = labels[0]
    zh_rows = jnp.transpose(zh_plane, (1, 0, 2))
    slot_ids = jnp.arange(capacity, dtype=jnp.int32)
    features = run_features(hw_plane, zh_rows, wz_plane, run_ids)
    validity = (slot_ids < run_total).astype(jnp.float32)
    dfeatures, weight_grads = decode(features, run_labels, validity, w_in, b_in, w_out, b_out)
    hw_local, zh_local, wz_local = plane_grads(dfeatures, run_ids, rows_blk, cols_blk)
    zh_grad = lax.psum_scatter(zh_local, "wa", scatter_dimension=0, tiled=True)
    wz_grad = lax.psum_scatter(wz_local, "ha", scatter_dimension=1, tiled=True)
    grad_w_in, grad_b_in, grad_w_out, grad_b_out = lax.psum(
        (weight_grads[0], weight_grads[1], weight_grads[2], weight_grads[3]), ("ha", "wa")
    )
    return (hw_local, zh_grad, wz_grad, grad_w_in, grad_b_in, grad_w_out, grad_b_out)


def solution(mesh):
    placed = (
        P("ha", "wa", None),
        P(None, "ha", None),
        P("wa", None, None),
        P(),
        P(),
        P(),
        P(),
        P(("ha", "wa"), None),
        P(("ha", "wa")),
        P(("ha", "wa"), None, None),
    )
    return jax.shard_map(
        local,
        mesh=mesh,
        in_specs=placed,
        out_specs=(
            P("ha", "wa", None),
            P("wa", "ha", None),
            P("wa", "ha", None),
            P(),
            P(),
            P(),
            P(),
        ),
        check_vma=False,
    )
```

profile of v0, /device:TPU:0, one launch (start us, length us, event | category | flops | bytes accessed | tf_op | source)
XLA Modules:
  0.0 623.7 jit_solution(4709305788778897297)
XLA Ops:
  10.3 13.4 %gather_fusion.1 = bf16[512,64,128]{2,1,0:T(8,128)(2,1)} fusion(bf16[32,64,128]{2,1,0:T(8,128)(2,1)S(1)} %bitcast.90, s32[1024]{0:T(1024)S(1)} %pad_clamp_fusion.1), kind=kCustom, calls=%fused_computation.1 | custom fusion | bytes 16779264 | tf_op jit(solution)/shard_map/gather | solution.py:55
  23.7 11.2 %convert_element_type.49 = f32[512,64,128]{2,1,0:T(8,128)} convert(bf16[512,64,128]{2,1,0:T(8,128)(2,1)} %gather_fusion.1) | non-fusion elementwise | flops 4194304 | bytes 25165824 | tf_op jit(solution)/shard_map/convert_element_type | solution.py:55
  35.0 2.6 gather_fusion
  40.4 13.9 %gather_fusion.2 = bf16[512,2,64,128]{3,2,1,0:T(8,128)(2,1)} fusion(bf16[64,2,64,128]{3,2,1,0:T(8,128)(2,1)S(1)} %bitcast.87, s32[1024]{0:T(1024)S(1)} %pad_clamp_fusion), kind=kCustom, calls=%fused_computation.2 | custom fusion | bytes 33556480 | tf_op jit(solution)/shard_map/gather | solution.py:56
  54.3 20.2 %add_convert_fusion = bf16[512,2,64,128]{3,2,1,0:T(8,128)(2,1)} fusion(bf16[512,2,64,128]{3,2,1,0:T(8,128)(2,1)} %gather_fusion.2, f32[512,64,128]{2,1,0:T(8,128)} %convert_element_type.49, f32[512,2,128]{2,1,0:T(2,128)S(1)} %convert_element_type.48), kind=kLoop, calls=%fused_computation.33 | loop fusion | flops 33554432 | bytes 50855936 | tf_op jit(solution)/shard_map/convert_element_type | solution.py:58
  74.5 197.7 %while.19 = (s32[]{:T(128)}, f32[128,256]{1,0:T(8,128)S(1)}, f32[256]{0:T(256)S(1)}, f32[256,18]{0,1:T(8,128)S(1)}, f32[18]{0:T(128)S(1)}, /*index=5*/f32[16,409...) while((s32[]{:T(128)}, f32[128,256]{1,0:T(8,128)S(1)}, ...), condition=%wide.region_5.6_spmd.clone, body=%wide.region_0.5_spmd.clone.sunk | while | flops 937407808 | bytes 35515956 | solution.py:99
  74.7 2.5 multiply_convert_fusion.4
  87.0 2.5 multiply_convert_fusion.4
  99.4 2.5 multiply_convert_fusion.4
  124.0 2.5 multiply_convert_fusion.4
  136.4 2.5 multiply_convert_fusion.4
  148.8 2.5 multiply_convert_fusion.4
  161.1 2.5 multiply_convert_fusion.4
  173.5 2.5 multiply_convert_fusion.4
  185.8 2.5 multiply_convert_fusion.4
  247.5 2.5 multiply_convert_fusion.4
  272.2 21.5 %fusion.11 = (f32[512,64,128]{2,1,0:T(8,128)}, f32[512,2,128]{2,1,0:T(2,128)S(1)}) fusion(f32[512,2,64,128]{3,2,1,0:T(8,128)} %bitcast.91), kind=kLoop, calls=%fused_computation.50 | loop fusion | flops 12451840 | bytes 50855936 | tf_op jit(solution)/shard_map/reduce_sum | solution.py:73
  293.8 51.9 %scatter_fusion.1 = f32[32,64,128]{2,1,0:T(8,128)S(1)} fusion(f32[32,64,128]{2,1,0:T(8,128)S(1)} %broadcast_in_dim.52, s32[512]{0:T(512)S(1)} %bitcast.105, f32[512,64,128]{2,1,0:T(8,128)} %get-tuple-element.146), kind=kCustom, calls=%fused_computation.4 | custom fusion | flops 4194304 | bytes 50333696 | tf_op jit(solution)/shard_map/scatter-add | solution.py:73
  346.8 2.6 broadcast_in_dim.53
  349.3 102.7 %scatter_fusion.2 = f32[64,2,64,128]{3,2,1,0:T(8,128)} fusion(f32[64,2,64,128]{3,2,1,0:T(8,128)} %broadcast_in_dim.53, s32[512]{0:T(512)S(1)} %bitcast.101, f32[512,2,64,128]{3,2,1,0:T(8,128)} %bitcast.92), kind=kCustom, calls=%fused_computation.5 | custom fusion | flops 8388608 | bytes 100665344 | tf_op jit(solution)/shard_map/scatter-add | solution.py:76
  452.0 6.5 %copy.25 = f32[128,64,128]{2,0,1:T(8,128)} copy(f32[128,64,128]{2,1,0:T(8,128)} %bitcast.88) | data formatting | bytes 8388608 | tf_op jit(solution)/shard_map/reshape | solution.py:77
  460.8 52.2 %scatter_fusion = f32[2048,2,128]{2,1,0:T(2,128)} fusion(f32[2048,2,128]{2,1,0:T(2,128)} %broadcast_in_dim.29, s32[512]{0:T(512)S(1)} %bitcast.103, f32[512,2,128]{2,1,0:T(2,128)S(1)} %get-tuple-element.147), kind=kCustom, calls=%fused_computation.3 | custom fusion | flops 131072 | bytes 1574912 | tf_op jit(solution)/shard_map/scatter-add | solution.py:68
  513.0 71.0 %all-reduce = (f32[256]{0:T(256)}, f32[256,18]{0,1:T(8,128)}, f32[18]{0:T(128)}) all-reduce(f32[256]{0:T(256)S(1)} %get-tuple-element.80, f32[256,18]{0,1:T(8,128)S(1)} %get-tuple-element.81, f32[18]{0:T(128)S(1)} %get-tuple-element.82), channel_id=1, replica_groups=mesh['ha'=16,'wa'=8] {'ha','wa'}, use_global_device_ids=true, to_apply=%region_14.15 | all-reduce | flops 4882 | bytes 39056 | tf_op jit(solution)/shard_map/psum | solution.py:119
  587.4 27.3 %all-reduce.3.cloned.1.call-done = f32[128,256]{1,0:T(8,128)} async-done(((f32[128,256]{1,0:T(8,128)}), f32[128,256]{1,0:T(8,128)}) %all-reduce.3.cloned.1.call-update) | async-done | bytes 131088 | tf_op jit(solution)/shard_map/psum | solution.py:119
  (267 shorter events, 184.3 us)
Async XLA Ops:
  8.0 32.4 %copy-start = (bf16[128,64,128]{2,1,0:T(8,128)(2,1)S(1)}, bf16[128,64,128]{2,1,0:T(8,128)(2,1)}, u32[]{:S(2)}) copy-start(bf16[128,64,128]{2,1,0:T(8,128)(2,1)} %param.14) | copy-start | bytes 6291460
  8.0 576.0 %reduce-scatter.3.cloned.1.call-start = ((), (), s32[]{:S(2)}) async-start(), calls=%async_computation.2 | async-start | bytes 1179648 | tf_op jit(solution)/shard_map/reduce_scatter | solution.py:117
  8.9 26.0 %copy-start.9 = (s32[512,1]{0,1:T(1,128)}, s32[512,1]{0,1:T(1,128)S(1)}, u32[]{:S(2)}) copy-start(s32[512,1]{0,1:T(1,128)S(1)} %get-tuple-element.187) | copy-start | bytes 6148
  9.0 14.7 %copy-start.7 = (s32[512,1]{0,1:T(1,128)}, s32[512,1]{0,1:T(1,128)S(1)}, u32[]{:S(2)}) copy-start(s32[512,1]{0,1:T(1,128)S(1)} %compare_select_fusion) | copy-start | bytes 6148
  54.3 20.2 %copy-start.5 = (bf16[128,256]{1,0:T(8,128)(2,1)S(1)}, bf16[128,256]{1,0:T(8,128)(2,1)}, u32[]{:S(2)}) copy-start(bf16[128,256]{1,0:T(8,128)(2,1)} %param.15) | copy-start | bytes 196612
  54.3 20.2 %copy-start.6 = (bf16[256,18]{0,1:T(8,128)(2,1)S(1)}, bf16[256,18]{0,1:T(8,128)(2,1)}, u32[]{:S(2)}) copy-start(bf16[256,18]{0,1:T(8,128)(2,1)} %param.17) | copy-start | bytes 27652
  54.3 20.2 %copy-start.11 = (f32[18]{0:T(128)S(1)}, f32[18]{0:T(128)}, u32[]{:S(2)}) copy-start(f32[18]{0:T(128)} %param.18) | copy-start | bytes 220
  54.3 20.2 %copy-start.12 = (f32[256]{0:T(256)S(1)}, f32[256]{0:T(256)}, u32[]{:S(2)}) copy-start(f32[256]{0:T(256)} %param.16) | copy-start | bytes 3076
  77.2 2.1 copy-start.3
  89.5 2.1 copy-start.3
  101.8 2.1 copy-start.3
  114.2 2.1 copy-start.3
  126.5 2.1 copy-start.3
  138.9 2.1 copy-start.3
  151.2 2.1 copy-start.3
  163.6 2.1 copy-start.3
  175.9 2.1 copy-start.3
  188.3 2.1 copy-start.3
  272.2 21.5 %copy-start.4 = (f32[128,256]{1,0:T(8,128)}, f32[128,256]{1,0:T(8,128)S(1)}, u32[]{:S(2)}) copy-start(f32[128,256]{1,0:T(8,128)S(1)} %get-tuple-element.79) | copy-start | bytes 393220
  345.7 3.6 copy-start.8
  346.7 238.9 %reduce-scatter.5.cloned.1.call-start = ((), (), s32[]{:S(2)}) async-start(), calls=%async_computation.3 | async-start | bytes 4456448 | tf_op jit(solution)/shard_map/reduce_scatter | solution.py:118
  458.6 2.2 copy-start.10
  458.6 157.6 %copy-start.1 = (bf16[128,64,128]{2,1,0:T(8,128)(2,1)S(1)}, bf16[128,64,128]{2,1,0:T(8,128)(2,1)}, u32[]{:S(2)}) copy-start(bf16[128,64,128]{2,1,0:T(8,128)(2,1)} %param.14) | copy-start | bytes 6291460
  458.6 156.0 %all-reduce.3.cloned.1.call-start = ((), (), s32[]{:S(2)}) async-start(), calls=%async_computation.4 | async-start | bytes 262144 | tf_op jit(solution)/shard_map/psum | solution.py:119
  (7 other events, 13.8 us)
Sparse Core Ops, SparseCore 0:
  346.8 41.7 reduce-scatter.2
  458.7 83.1 reduce-scatter.4
Sparse Core Ops, SparseCore 1:
  465.1 149.5 all-reduce.2
where the time goes:
time: 630 us; the launch traced here: 624 us
  other arithmetic  284 us (45%)
  matrix products  173 us (27%)
  blocking collectives  71 us (11%)
  local copies, waits for them, and re-layouts  50.4 us (8%)
  waiting for transfers between devices  27.8 us (4%)
  between operations  16.3 us (3%)
    scatter-add x1, other arithmetic, plane_grads(): jnp.zeros((pair_cols, 2, depth_z, channels), jnp.float32).at[run_pair]  103 us
    psum x1, blocking collectives, local(): lax.psum((weight_grads[0], weight_grads[1], weight_grads[2], weight_grads...  71 us
    dot_general x32, matrix products, contract_cols(): lax.dot_general(left, right, (((1,), (1,)), ((), ())), preferred_element_...  61.7 us
    dot_general x32, matrix products, contract_rows(): lax.dot_general(left, right, (((0,), (0,)), ((), ())), preferred_element_...  61.1 us
    scatter-add x1, other arithmetic, plane_grads(): hw_local.at[run_ids].add(jnp.sum(dfeatures, axis=2))  52.2 us
    scatter-add x1, other arithmetic, plane_grads(): zh_rows_grad = jnp.zeros((rows_blk, depth_z, channels), jnp.float32).at[r...  51.9 us
    dot_general x16, matrix products, sample_grads(): preact = jnp.dot(features, w_in, preferred_element_type=jnp.float32) + b_in  39.6 us
    psum x1, waiting for transfers between devices, local(): lax.psum((weight_grads[0], weight_grads[1], weight_grads[2], weight_grads...  27.3 us
  transfers between devices with their start and end apart: 3, of which 1 were waited for; matrix products, arithmetic and copies ran while one was open for 27% of the time, Pallas kernels for 0%

commit v1 on v0

v1 whole, which is shorter than its diff:
```python
import functools

import jax
import jax.numpy as jnp
from jax import lax
from jax.experimental import pallas as pl
from jax.experimental.pallas import tpu as pltpu
from jax.sharding import PartitionSpec as P

F32 = jnp.float32
BF16 = jnp.bfloat16
GRAD_SCALE = 0.25
GROUP = 16
CLS = 32


def dotg(left, right, dims):
    return lax.dot_general(left, right, ((dims[0], dims[1]), ((), ())), preferred_element_type=F32)


def decode_kernel(
    ids_ref, count_ref, hw_ref, zh_ref, wz_ref, labels_ref, win_ref, bin_ref, wout_ref, bout_ref,
    hw_out, zh_out, wz_out, gwi_ref, gwo_ref, gbo_ref,
    hw32,
):
    rows, depth, chans = zh_ref.shape
    pairs = wz_ref.shape[0]
    used = count_ref[0]
    hw32[...] = hw_ref[...].astype(F32)
    hw_out[...] = jnp.zeros_like(hw_out)
    zh_out[...] = jnp.zeros_like(zh_out)
    wz_out[...] = jnp.zeros_like(wz_out)
    gwi_ref[...] = jnp.zeros_like(gwi_ref)
    gwo_ref[...] = jnp.zeros_like(gwo_ref)
    gbo_ref[...] = jnp.zeros_like(gbo_ref)
    samples = GROUP * 2 * depth
    run = 2 * depth

    def body(step, carry):
        base = step * GROUP
        spots = []
        parts = []
        for g in range(GROUP):
            rid = ids_ref[base + g]
            row = rid // pairs
            pair = rid % pairs
            spots.append((rid, row, pair))
            zh = zh_ref[row].astype(F32)
            for p in range(2):
                hw = hw32[pl.ds(2 * rid + p, 1), :]
                wz = wz_ref[pair, p * depth:(p + 1) * depth, :].astype(F32)
                parts.append(((hw + zh) + wz).astype(BF16))
        feats = jnp.concatenate(parts, axis=0)
        u = jnp.dot(feats, win_ref[...] * 0.5, preferred_element_type=F32) + bin_ref[...]
        a = jnp.tanh(u) + 1.0
        h = u * a
        hid = h.astype(BF16)
        logits = dotg(wout_ref[...], hid, ((1,), (1,)))
        dparts = []
        for g in range(GROUP):
            lt = logits[:, g * run:(g + 1) * run] + bout_ref[...]
            top = jnp.max(lt, axis=0, keepdims=True)
            e = jnp.exp(lt - top)
            inv = 1.0 / jnp.sum(e, axis=0, keepdims=True)
            lab = labels_ref[pl.ds(base + g, 1), :]
            cls = lax.broadcasted_iota(jnp.int32, lt.shape, 0)
            hot = jnp.where(cls == lab, 1.0, 0.0)
            scale = jnp.where(base + g < used, GRAD_SCALE, 0.0)
            dparts.append(((e * inv - hot) * scale).astype(BF16))
        dlt = jnp.concatenate(dparts, axis=1)
        gwo_ref[...] += jnp.dot(dlt, hid, preferred_element_type=F32)
        tot = dparts[0].astype(F32)
        for g in range(1, GROUP):
            tot += dparts[g].astype(F32)
        gbo_ref[...] += tot
        dhh = dotg(dlt, wout_ref[...] * 0.5, ((0,), (0,)))
        q = (u + u + 1.0) - h
        dpre = (dhh * a * q).astype(BF16)
        lhs = jnp.concatenate([feats.T, jnp.ones((16, samples), BF16)], axis=0)
        gwi_ref[...] += jnp.dot(lhs, dpre, preferred_element_type=F32)
        df = dotg(dpre, win_ref[...], ((1,), (1,)))
        for g in range(GROUP):
            rid, row, pair = spots[g]
            d = df[g * run:(g + 1) * run]
            wz_out[pair] += d
            zh_out[row] += d[:depth] + d[depth:]
            for p in range(2):
                hw_out[pl.ds(2 * rid + p, 1), :] = jnp.sum(d[p * depth:(p + 1) * depth], axis=0, keepdims=True)
        return carry

    lax.fori_loop(0, pl.cdiv(used, GROUP), body, 0)


def decode_runs(ids, count, hw, zh, wz, labels, w_in, b_in, w_out, b_out):
    rows, depth, chans = zh.shape
    pairs = wz.shape[0]
    hid, ncls = w_out.shape
    hw_rows = hw.shape[0]
    wout = jnp.zeros((CLS, hid), BF16).at[:ncls].set(w_out.T)
    bout = jnp.full((CLS, 1), -1e30, F32).at[:ncls, 0].set(b_out)
    smem = pl.BlockSpec(memory_space=pltpu.SMEM)
    vmem = pl.BlockSpec(memory_space=pltpu.VMEM)
    return pl.pallas_call(
        decode_kernel,
        out_shape=(
            jax.ShapeDtypeStruct((hw_rows, chans), F32),
            jax.ShapeDtypeStruct((rows, depth, chans), F32),
            jax.ShapeDtypeStruct((pairs, 2 * depth, chans), F32),
            jax.ShapeDtypeStruct((chans + 16, hid), F32),
            jax.ShapeDtypeStruct((CLS, hid), F32),
            jax.ShapeDtypeStruct((CLS, 2 * depth), F32),
        ),
        in_specs=[smem, smem] + [vmem] * 8,
        out_specs=[vmem] * 6,
        scratch_shapes=[pltpu.VMEM((hw_rows, chans), F32)],
        compiler_params=pltpu.CompilerParams(vmem_limit_bytes=48 * 1024 * 1024),
    )(ids, count, hw, zh, wz, labels, w_in, (0.5 * b_in).reshape(1, hid), wout, bout)


def local(hw_plane, zh_plane, wz_plane, w_in, b_in, w_out, b_out, run_index, run_count, labels):
    rows, cols, chans = hw_plane.shape
    depth = zh_plane.shape[0]
    ncls = w_out.shape[1]
    zh_rows = jnp.transpose(zh_plane, (1, 0, 2))
    hw, zh, wz, gwi, gwo, gbo = decode_runs(
        run_index[0], run_count, hw_plane.reshape(rows * cols, chans), zh_rows,
        wz_plane.reshape(cols // 2, 2 * depth, chans), labels[0], w_in, b_in, w_out, b_out,
    )
    zh_grad = lax.psum_scatter(jnp.transpose(zh, (1, 0, 2)), "wa", scatter_dimension=0, tiled=True)
    wz_grad = lax.psum_scatter(wz.reshape(cols, depth, chans), "ha", scatter_dimension=1, tiled=True)
    gwi, gwo, gbo = lax.psum((gwi, gwo, jnp.sum(gbo, axis=1)), ("ha", "wa"))
    return (hw.reshape(rows, cols, chans), zh_grad, wz_grad, gwi[:chans], gwi[chans], gwo[:ncls].T, gbo[:ncls])


def solution(mesh):
    placed = (
        P("ha", "wa", None),
        P(None, "ha", None),
        P("wa", None, None),
        P(),
        P(),
        P(),
        P(),
        P(("ha", "wa"), None),
        P(("ha", "wa")),
        P(("ha", "wa"), None, None),
    )
    return jax.shard_map(
        local,
        mesh=mesh,
        in_specs=placed,
        out_specs=(P("ha", "wa", None), P("wa", "ha", None), P("wa", "ha", None), P(), P(), P(), P()),
        check_vma=False,
    )
```

time: 630 us -> 246 us (0.39)
  other arithmetic: 284 us -> 0.79 us
  matrix products: 173 us -> 0 us
  Pallas kernels: 0 us -> 63 us
  waiting for transfers between devices: 27.8 us -> 76.9 us
  local copies, waits for them, and re-layouts: 50.4 us -> 21.4 us
    scatter-add x3 -> x0, other arithmetic: 207 us -> none  [the longest x1 103 us: plane_grads(): jnp.zeros((pair_cols, 2, depth_z, channels), jnp.float32).at[run_pair]]
    dot_general x96 -> x0, matrix products: 173 us -> none  [the longest x32 61.7 us: contract_cols(): lax.dot_general(left, right, (((1,), (1,)), ((), ())), preferred_element_...]
    pallas_call x0 -> x1, Pallas kernels: none -> 63 us  [decode_runs(): pl.pallas_call(decode_kernel, out_shape=(jax.ShapeDtypeStruct((hw_rows, c...]
    psum x1, waiting for transfers between devices: 27.3 us -> 76.3 us  [local(): gwi, gwo, gbo = lax.psum((gwi, gwo, jnp.sum(gbo, axis=1)), ('ha', 'wa'))]
    convert_element_type x4 -> x0, other arithmetic: 31.6 us -> none  [the longest x1 20.2 us: run_features(): return summed.astype(jnp.bfloat16)]
    gather x3 -> x0, local copies, waits for them, and re-layouts: 29.9 us -> none  [the longest x1 13.9 us: run_features(): wz_block.reshape(pair_cols, 2, depth_z, channels)[run_pair]]
    reduce_sum x33 -> x1, other arithmetic: 26.8 us -> 0.11 us  [local(): gwi, gwo, gbo = lax.psum((gwi, gwo, jnp.sum(gbo, axis=1)), ('ha', 'wa'))]
    mul x16 -> x1, other arithmetic: 17.1 us -> 0.68 us  [decode_runs(): 0.5 * b_in]
  transfers between devices with their start and end apart: 3 -> 3, of which waited for: 1 -> 1; matrix products, arithmetic and copies ran while one was open for 27% -> 5% of each run, Pallas kernels for 0% -> 0%
where the time goes in v1:
time: 246 us; the launch traced here: 245 us
  waiting for transfers between devices  76.9 us (31%)
  blocking collectives  67.1 us (27%)
  Pallas kernels  63 us (26%)
  local copies, waits for them, and re-layouts  21.4 us (9%)
  between operations  16.1 us (7%)
    psum x1, waiting for transfers between devices, local(): gwi, gwo, gbo = lax.psum((gwi, gwo, jnp.sum(gbo, axis=1)), ('ha', 'wa'))  76.3 us
    psum x1, blocking collectives, local(): gwi, gwo, gbo = lax.psum((gwi, gwo, jnp.sum(gbo, axis=1)), ('ha', 'wa'))  67.1 us
    pallas_call x1, Pallas kernels, decode_runs(): pl.pallas_call(decode_kernel, out_shape=(jax.ShapeDtypeStruct((hw_rows, c...  63 us
    unnamed x13, local copies, waits for them, and re-layouts  9.94 us
    reshape x1, local copies, waits for them, and re-layouts, local(): wz.reshape(cols, depth, chans)  6.55 us
  transfers between devices with their start and end apart: 3, of which 1 were waited for; matrix products, arithmetic and copies ran while one was open for 5% of the time, Pallas kernels for 0%

profile of v1, /device:TPU:0, one launch (start us, length us, event | category | flops | bytes accessed | tf_op | source)
XLA Modules:
  0.0 245.4 jit_solution(2557401717748781333)
XLA Ops:
  8.0 0.0 all-reduce.5.cloned.1.call-start
  8.7 0.7 broadcast_multiply_fusion
  9.4 0.7 copy.21
  10.1 1.2 copy.26
  11.4 0.7 scatter.6.wout_ref
  12.1 1.6 copy-done
  13.7 1.2 copy-done.1
  14.9 0.9 copy-done.2
  15.9 0.8 copy-done.3
  16.7 0.7 copy-done.4
  17.4 63.0 %shard_map.153 = (f32[4096,128]{1,0:T(8,128)}, f32[32,64,128]{2,1,0:T(8,128)}, f32[64,128,128]{2,1,0:T(8,128)}, f32[144,256]{1,0:T(8,128)}, f32[32,256]{1,0:T(8,128)S(1)}, /*index=5*/f32[32,128]{1,0:T(8,128)S(1)}) custom-call(s32[512]{0:T(512)S(1)} %bitcast.22, s32[1]{0:T(128)S(6)} %copy.28.count_ref, bf16[4096,128]{1,0:T(8,128)(2,1)S(1)} %bitcast.19, ...), custom_call_target="tpu_custom_call" | custom-call | tf_op jit(solution)/shard_map/pallas_call | solution.py:103
  80.4 0.0 reduce-scatter.3.cloned.1.call-start
  80.5 0.5 reduce-scatter.3.cloned.1.call-update
  81.0 0.0 reduce-scatter.5.cloned.1.call-start
  81.0 6.6 %copy.22 = f32[128,64,128]{2,0,1:T(8,128)} copy(f32[128,64,128]{2,1,0:T(8,128)} %bitcast.23) | data formatting | bytes 8388608 | tf_op jit(solution)/shard_map/reshape | solution.py:130
  87.6 0.0 reduce-scatter.5.cloned.1.call-update
  87.6 0.1 reduce_sum.9
  87.7 67.1 %all-reduce.2 = (f32[32,256]{1,0:T(8,128)S(1)}, f32[32]{0:T(128)}) all-reduce(f32[32,256]{1,0:T(8,128)S(1)} %get-tuple-element.41, f32[32]{0:T(128)S(1)} %reduce_sum.9), channel_id=1, replica_groups=mesh['ha'=16,'wa'=8] {'ha','wa'}, use_global_device_ids=true, to_apply=%region_3.0 | all-reduce | flops 8224 | bytes 65792 | tf_op jit(solution)/shard_map/psum | solution.py:131
  154.8 0.6 slice_bitcast_fusion
  155.4 76.3 %all-reduce.5.cloned.1.call-done = f32[144,256]{1,0:T(8,128)} async-done(((f32[144,256]{1,0:T(8,128)}), f32[144,256]{1,0:T(8,128)}) %all-reduce.5.cloned.1.call-update) | async-done | bytes 147472 | tf_op jit(solution)/shard_map/psum | solution.py:131
  231.8 1.3 slice.49
  233.0 1.6 slice.48
  234.6 1.6 copy.23
  236.2 1.8 copy.24
  (9 shorter events, 0.0 us)
Async XLA Ops:
  8.0 223.8 %all-reduce.5.cloned.1.call-start = ((), (), s32[]{:S(2)}) async-start(), calls=%async_computation.4 | async-start | bytes 294912 | tf_op jit(solution)/shard_map/psum | solution.py:131
  12.1 1.6 copy-start
  13.7 1.2 copy-start.1
  14.9 0.9 copy-start.2
  15.9 0.8 copy-start.3
  16.7 0.7 copy-start.4
  80.4 154.2 %reduce-scatter.3.cloned.1.call-start = ((), (), s32[]{:S(2)}) async-start(), calls=%async_computation.2 | async-start | bytes 1179648 | tf_op jit(solution)/shard_map/reduce_scatter | solution.py:129
  81.0 155.2 %reduce-scatter.5.cloned.1.call-start = ((), (), s32[]{:S(2)}) async-start(), calls=%async_computation.3 | async-start | bytes 4456448 | tf_op jit(solution)/shard_map/reduce_scatter | solution.py:130
Sparse Core Ops, SparseCore 0:
  80.5 151.1 all-reduce.4
Sparse Core Ops, SparseCore 1:
  83.3 38.7 reduce-scatter.2
  126.0 79.0 reduce-scatter.4

commit v2 on v1

--- a/solution.py
+++ b/solution.py
@@ -12,6 +12,8 @@
 GRAD_SCALE = 0.25
 GROUP = 16
 CLS = 32
+CHUNKS = 4
+MESH = pl.DeviceIdType.MESH
 
 
 def dotg(left, right, dims):
@@ -20,8 +22,8 @@
 
 def decode_kernel(
     ids_ref, count_ref, hw_ref, zh_ref, wz_ref, labels_ref, win_ref, bin_ref, wout_ref, bout_ref,
-    hw_out, zh_out, wz_out, gwi_ref, gwo_ref, gbo_ref,
-    hw32,
+    hw_out, zh_out, wz_out, wt_out,
+    hw32, gwi_ref, gwo_ref, gbo_ref,
 ):
     rows, depth, chans = zh_ref.shape
     pairs = wz_ref.shape[0]
@@ -82,13 +84,19 @@
         for g in range(GROUP):
             rid, row, pair = spots[g]
             d = df[g * run:(g + 1) * run]
-            wz_out[pair] += d
-            zh_out[row] += d[:depth] + d[depth:]
+            zh_out[:, row] += (d[:depth] + d[depth:]).reshape(depth // 8, 8, chans)
             for p in range(2):
+                wz_out[:, 2 * pair + p] += d[p * depth:(p + 1) * depth].reshape(depth // 8, 8, chans)
                 hw_out[pl.ds(2 * rid + p, 1), :] = jnp.sum(d[p * depth:(p + 1) * depth], axis=0, keepdims=True)
         return carry
 
     lax.fori_loop(0, pl.cdiv(used, GROUP), body, 0)
+    top = chans + 16
+    wt_out[0:top] = gwi_ref[:, :128]
+    wt_out[top:2 * top] = gwi_ref[:, 128:]
+    wt_out[2 * top:2 * top + CLS] = gwo_ref[:, :128]
+    wt_out[2 * top + CLS:2 * top + 2 * CLS] = gwo_ref[:, 128:]
+    wt_out[2 * top + 2 * CLS:] = gbo_ref[...]
 
 
 def decode_runs(ids, count, hw, zh, wz, labels, w_in, b_in, w_out, b_out):
@@ -104,17 +112,258 @@
         decode_kernel,
         out_shape=(
             jax.ShapeDtypeStruct((hw_rows, chans), F32),
-            jax.ShapeDtypeStruct((rows, depth, chans), F32),
-            jax.ShapeDtypeStruct((pairs, 2 * depth, chans), F32),
-            jax.ShapeDtypeStruct((chans + 16, hid), F32),
-            jax.ShapeDtypeStruct((CLS, hid), F32),
-            jax.ShapeDtypeStruct((CLS, 2 * depth), F32),
+            jax.ShapeDtypeStruct((depth // 8, rows, 8, chans), F32),
+            jax.ShapeDtypeStruct((depth // 8, 2 * pairs, 8, chans), F32),
+            jax.ShapeDtypeStruct((2 * (chans + 16) + 3 * CLS, chans), F32),
         ),
         in_specs=[smem, smem] + [vmem] * 8,
-        out_specs=[vmem] * 6,
-        scratch_shapes=[pltpu.VMEM((hw_rows, chans), F32)],
+        out_specs=[vmem] * 4,
+        scratch_shapes=[
+            pltpu.VMEM((hw_rows, chans), F32),
+            pltpu.VMEM((chans + 16, hid), F32),
+            pltpu.VMEM((CLS, hid), F32),
+            pltpu.VMEM((CLS, 2 * depth), F32),
+        ],
         compiler_params=pltpu.CompilerParams(vmem_limit_bytes=48 * 1024 * 1024),
     )(ids, count, hw, zh, wz, labels, w_in, (0.5 * b_in).reshape(1, hid), wout, bout)
+
+
+def ring_copies(src, chain_p, chain_m, final, sems, axis, me, size, span, at):
+    plus, minus, far = lax.rem(me + 1, size), lax.rem(me + 3, size), lax.rem(me + 2, size)
+    half = span // 2
+    lo, hi = pl.ds(at, half), pl.ds(at + half, half)
+
+    def copy(i, source, dest, to):
+        return pltpu.make_async_remote_copy(
+            src_ref=source, dst_ref=dest, send_sem=sems.at[0, i], recv_sem=sems.at[1, i],
+            device_id=axis(to), device_id_type=MESH)
+
+    first = [
+        copy(0, src.at[:, far, lo], chain_p, plus),
+        copy(1, src.at[:, far, hi], chain_m, minus),
+        copy(2, src.at[:, minus, lo], final.at[1, :, 0:half], minus),
+        copy(3, src.at[:, plus, hi], final.at[1, :, half:span], plus),
+    ]
+    second = [
+        copy(4, chain_p, final.at[0, :, 0:half], plus),
+        copy(5, chain_m, final.at[0, :, half:span], minus),
+    ]
+
+    def relay():
+        first[0].wait_recv()
+        chain_p[...] += src[:, plus, lo]
+        second[0].start()
+        first[1].wait_recv()
+        chain_m[...] += src[:, minus, hi]
+        second[1].start()
+
+    def finish():
+        for c in (first[2], first[3], second[0], second[1]):
+            c.wait_recv()
+        return final[0] + final[1] + src[:, me, pl.ds(at, span)]
+
+    def done():
+        for c in first + second:
+            c.wait_send()
+
+    return first, relay, finish, done
+
+
+def reduce_kernel(
+    wz_ref, zh_ref, wt_ref, wz_out, zh_out, wt_out,
+    core_in, xchain_p, xchain_m, xfinal, xsum, yin, swap,
+    zchain_p, zchain_m, zfinal, zsum, zin, zres, wt_in, wt_mid,
+    core_sem, x_sem, y_sem, swap_sem, z_sem, yl_sem, wa_sem, wb_sem, wc_sem,
+):
+    ha, wa = lax.axis_index("ha"), lax.axis_index("wa")
+    yh, x, c = ha // 8, lax.rem(ha // 2, 4), lax.rem(ha, 2)
+    yl, z = wa // 4, lax.rem(wa, 4)
+    half_w = wz_ref.shape[2] // 2
+    span = half_w // CHUNKS
+    n_ha, n_wa = wt_ref.shape[0], 8
+
+    def on_x(to):
+        return (yh * 8 + to * 2 + c, wa)
+
+    def on_z(to):
+        return (ha, yl * 4 + to)
+
+    sibling = (ha + 1 - 2 * c, wa)
+    across = (lax.rem(ha + 8, 16), wa)
+    beside = (ha, lax.rem(wa + 4, 8))
+
+    barrier = pltpu.get_barrier_semaphore()
+
+    def greet_ha(i, carry):
+        pl.semaphore_signal(barrier, inc=1, device_id=(lax.rem(ha + i, n_ha), wa), device_id_type=MESH)
+        return carry
+
+    def greet_wa(i, carry):
+        pl.semaphore_signal(barrier, inc=1, device_id=(ha, lax.rem(wa + i, n_wa)), device_id_type=MESH)
+        return carry
+
+    lax.fori_loop(1, n_ha, greet_ha, 0)
+    lax.fori_loop(1, n_wa, greet_wa, 0)
+    pl.semaphore_wait(barrier, n_ha + n_wa - 2)
+
+    def send(source, dest, sems, to):
+        return pltpu.make_async_remote_copy(
+            src_ref=source, dst_ref=dest, send_sem=sems.at[0], recv_sem=sems.at[1],
+            device_id=to, device_id_type=MESH)
+
+    core = [
+        send(wz_ref.at[:, :, pl.ds((1 - c) * half_w + k * span, span)], core_in.at[:, :, pl.ds(k * span, span)],
+             core_sem.at[k], sibling)
+        for k in range(CHUNKS)
+    ]
+    for k in range(CHUNKS):
+        core[k].start()
+    zring = ring_copies(zh_ref, zchain_p, zchain_m, zfinal, z_sem, on_z, z, 4, zh_ref.shape[2], 0)
+    for cp in zring[0]:
+        cp.start()
+
+    def wt_first(i):
+        to = lax.rem(ha + i, n_ha)
+        return pltpu.make_async_remote_copy(
+            src_ref=wt_ref.at[to], dst_ref=wt_in.at[ha], send_sem=wa_sem.at[0, to], recv_sem=wa_sem.at[1, ha],
+            device_id=(to, wa), device_id_type=MESH)
+
+    def wt_second(i):
+        to = lax.rem(wa + i, n_wa)
+        return pltpu.make_async_remote_copy(
+            src_ref=wt_mid.at[wa], dst_ref=wt_mid.at[wa], send_sem=wb_sem.at[0, to], recv_sem=wb_sem.at[1, wa],
+            device_id=(ha, to), device_id_type=MESH)
+
+    def wt_third(i):
+        to = lax.rem(ha + i, n_ha)
+        return pltpu.make_async_remote_copy(
+            src_ref=wt_out.at[ha], dst_ref=wt_out.at[ha], send_sem=wc_sem.at[0, to], recv_sem=wc_sem.at[1, ha],
+            device_id=(to, wa), device_id_type=MESH)
+
+    def start(make, n):
+        def go(i, carry):
+            make(i).start()
+            return carry
+        lax.fori_loop(1, n, go, 0)
+
+    def wait_send(make, n):
+        def go(i, carry):
+            make(i).wait_send()
+            return carry
+        lax.fori_loop(1, n, go, 0)
+
+    def wait_slot(buf, sems, me, n, own):
+        def go(i, carry):
+            frm = lax.rem(me + i, n)
+            pltpu.make_async_remote_copy(
+                src_ref=buf.at[frm], dst_ref=buf.at[frm], send_sem=sems.at[0, frm], recv_sem=sems.at[1, frm],
+                device_id=own, device_id_type=MESH).wait_recv()
+            return carry
+        lax.fori_loop(1, n, go, 0)
+
+    start(wt_first, n_ha)
+    rings = []
+    for k in range(CHUNKS):
+        rows = pl.ds(k * span, span)
+        core[k].wait_recv()
+        core_in[:, :, rows] += wz_ref[:, :, pl.ds(c * half_w + k * span, span)]
+        ring = ring_copies(core_in, xchain_p.at[k], xchain_m.at[k], xfinal.at[k], x_sem.at[k], on_x, x, 4, span, k * span)
+        for cp in ring[0]:
+            cp.start()
+        rings.append(ring)
+    zring[1]()
+    wait_slot(wt_in, wa_sem, ha, n_ha, sibling)
+    wt_in[ha] = wt_ref[ha]
+    tot = wt_in[0]
+    for i in range(1, n_ha):
+        tot += wt_in[i]
+    wt_mid[wa] = tot
+    start(wt_second, n_wa)
+    for k in range(CHUNKS):
+        rings[k][1]()
+    zsum[...] = zring[2]()
+    to_beside = send(zsum.at[1 - yl], zin, yl_sem, beside)
+    to_beside.start()
+    ys = []
+    for k in range(CHUNKS):
+        rows = pl.ds(k * span, span)
+        xsum[:, rows] = rings[k][2]()
+        ys.append(send(xsum.at[1 - yh, rows], yin.at[rows], y_sem.at[k], across))
+        ys[k].start()
+    wait_slot(wt_mid, wb_sem, wa, n_wa, beside)
+    tot = wt_mid[0]
+    for i in range(1, n_wa):
+        tot += wt_mid[i]
+    wt_out[ha] = tot
+    start(wt_third, n_ha)
+    to_beside.wait_recv()
+    zres[...] = zsum[yl] + zin[...]
+    for i in range(8):
+        zh_out[i] = zres[:, i, :]
+    swaps = []
+    for k in range(CHUNKS):
+        rows = pl.ds(k * span, span)
+        ys[k].wait_recv()
+        r = xsum[yh, rows] + yin[rows]
+        mine = pl.ds(c * half_w + k * span, span)
+        wz_out[mine] = jnp.where(c == 0, r[:, :4], r[:, 4:])
+        swap[rows] = jnp.where(c == 0, r[:, 4:], r[:, :4])
+        swaps.append(send(swap.at[rows], wz_out.at[mine], swap_sem.at[k], sibling))
+        swaps[k].start()
+    for k in range(CHUNKS):
+        swaps[k].wait_recv()
+    wait_slot(wt_out, wc_sem, ha, n_ha, sibling)
+    for k in range(CHUNKS):
+        core[k].wait_send()
+        rings[k][3]()
+        ys[k].wait_send()
+        swaps[k].wait_send()
+    zring[3]()
+    to_beside.wait_send()
+    wait_send(wt_first, n_ha)
+    wait_send(wt_second, n_wa)
+    wait_send(wt_third, n_ha)
+
+
+def reduce_all(wz, zh, wt):
+    width, chans = wz.shape[2], wz.shape[4]
+    rows = zh.shape[2]
+    half_w = width // 2
+    span = half_w // CHUNKS
+    vmem = pl.BlockSpec(memory_space=pltpu.VMEM)
+    buf = lambda *s: pltpu.VMEM(s, F32)
+    dma = lambda *s: pltpu.SemaphoreType.DMA(s)
+    return pl.pallas_call(
+        reduce_kernel,
+        out_shape=(
+            jax.ShapeDtypeStruct((width, 4, chans), F32),
+            jax.ShapeDtypeStruct((8, rows, chans), F32),
+            jax.ShapeDtypeStruct(wt.shape, F32),
+        ),
+        in_specs=[vmem] * 3,
+        out_specs=[vmem] * 3,
+        scratch_shapes=[
+            buf(2, 4, half_w, 8, chans),
+            buf(CHUNKS, 2, span // 2, 8, chans),
+            buf(CHUNKS, 2, span // 2, 8, chans),
+            buf(CHUNKS, 2, 2, span, 8, chans),
+            buf(2, half_w, 8, chans),
+            buf(half_w, 8, chans),
+            buf(half_w, 4, chans),
+            buf(2, rows // 2, 8, chans),
+            buf(2, rows // 2, 8, chans),
+            buf(2, 2, rows, 8, chans),
+            buf(2, rows, 8, chans),
+            buf(rows, 8, chans),
+            buf(rows, 8, chans),
+            buf(*wt.shape),
+            buf(8, *wt.shape[1:]),
+            dma(CHUNKS, 2), dma(CHUNKS, 2, 6), dma(CHUNKS, 2), dma(CHUNKS, 2), dma(2, 6), dma(2),
+            dma(2, 16), dma(2, 8), dma(2, 16),
+        ],
+        compiler_params=pltpu.CompilerParams(
+            collective_id=0, has_side_effects=True, vmem_limit_bytes=48 * 1024 * 1024),
+    )(wz, zh, wt)
 
 
 def local(hw_plane, zh_plane, wz_plane, w_in, b_in, w_out, b_out, run_index, run_count, labels):
@@ -122,14 +371,19 @@
     depth = zh_plane.shape[0]
     ncls = w_out.shape[1]
     zh_rows = jnp.transpose(zh_plane, (1, 0, 2))
-    hw, zh, wz, gwi, gwo, gbo = decode_runs(
+    hw, zh, wz, wt = decode_runs(
         run_index[0], run_count, hw_plane.reshape(rows * cols, chans), zh_rows,
         wz_plane.reshape(cols // 2, 2 * depth, chans), labels[0], w_in, b_in, w_out, b_out,
     )
-    zh_grad = lax.psum_scatter(jnp.transpose(zh, (1, 0, 2)), "wa", scatter_dimension=0, tiled=True)
-    wz_grad = lax.psum_scatter(wz.reshape(cols, depth, chans), "ha", scatter_dimension=1, tiled=True)
-    gwi, gwo, gbo = lax.psum((gwi, gwo, jnp.sum(gbo, axis=1)), ("ha", "wa"))
-    return (hw.reshape(rows, cols, chans), zh_grad, wz_grad, gwi[:chans], gwi[chans], gwo[:ncls].T, gbo[:ncls])
+    wz_grad, zh_grad, wt = reduce_all(
+        wz.reshape(2, 4, cols, 8, chans), zh.reshape(2, 4, rows, 8, chans), wt.reshape(16, -1, chans))
+    wt = wt.reshape(-1, chans)
+    top = chans + 16
+    gwi = jnp.concatenate([wt[:chans], wt[top:top + chans]], axis=1)
+    gbi = jnp.concatenate([wt[chans], wt[top + chans]])
+    gwo = jnp.concatenate([wt[2 * top:2 * top + ncls], wt[2 * top + CLS:2 * top + CLS + ncls]], axis=1).T
+    gbo = jnp.sum(wt[2 * top + 2 * CLS:2 * top + 2 * CLS + ncls], axis=1)
+    return (hw.reshape(rows, cols, chans), zh_grad, wz_grad, gwi, gbi, gwo, gbo)
 
 
 def solution(mesh):

time: 246 us -> 117 us (0.48)
  waiting for transfers between devices: 76.9 us -> 0 us
  blocking collectives: 67.1 us -> 0 us
  Pallas kernels: 63 us -> 99.1 us
  between operations: 16.1 us -> 1.32 us
  local copies, waits for them, and re-layouts: 21.4 us -> 11.5 us
    psum x1 -> x0, waiting for transfers between devices: 76.3 us -> none  [local(): gwi, gwo, gbo = lax.psum((gwi, gwo, jnp.sum(gbo, axis=1)), ('ha', 'wa'))]
    psum x1 -> x0, blocking collectives: 67.1 us -> none  [local(): gwi, gwo, gbo = lax.psum((gwi, gwo, jnp.sum(gbo, axis=1)), ('ha', 'wa'))]
    pallas_call x0 -> x1, Pallas kernels: none -> 35.8 us  [reduce_all(): pl.pallas_call(reduce_kernel, out_shape=(jax.ShapeDtypeStruct((width, 4,...]
    reshape x1 -> x0, local copies, waits for them, and re-layouts: 6.55 us -> none  [local(): wz.reshape(cols, depth, chans)]
    slice x2 -> x1, local copies, waits for them, and re-layouts: 2.83 us -> 0.01 us  [local(): gwi = jnp.concatenate([wt[:chans], wt[top:top + chans]], axis=1)]
    unnamed x13 -> x15, local copies, waits for them, and re-layouts: 9.94 us -> 10.1 us
  transfers between devices with their start and end apart: 3 -> 0, of which waited for: 1 -> 0; matrix products, arithmetic and copies ran while one was open for 5% -> 0% of each run, Pallas kernels for 0% -> 0%
where the time goes in v2:
time: 117 us; the launch traced here: 115 us
  Pallas kernels  99.1 us (85%)
  local copies, waits for them, and re-layouts  11.5 us (10%)
  other arithmetic  3.15 us (3%)
  between operations  1.32 us (1%)
    pallas_call x1, Pallas kernels, decode_runs(): pl.pallas_call(decode_kernel, out_shape=(jax.ShapeDtypeStruct((hw_rows, c...  63.3 us
    pallas_call x1, Pallas kernels, reduce_all(): pl.pallas_call(reduce_kernel, out_shape=(jax.ShapeDtypeStruct((width, 4,...  35.8 us
    unnamed x15, local copies, waits for them, and re-layouts  10.1 us

profile of v2, /device:TPU:0, one launch (start us, length us, event | category | flops | bytes accessed | tf_op | source)
XLA Modules:
  0.0 115.1 jit_solution(4195579574085230396)
XLA Ops:
  1.3 0.7 broadcast_multiply_fusion
  2.0 0.7 copy.18
  2.7 0.7 scatter.6.wout_ref
  3.4 1.2 %copy.20 = bf16[64,32,128]{2,0,1:T(8,128)(2,1)S(1)} copy(bf16[64,32,128]{2,1,0:T(8,128)(2,1)} %param.15) | data formatting | bytes 1048576 | tf_op args[1]
  4.7 0.0 copy-start.1
  4.7 1.6 %copy-done.1 = bf16[128,64,128]{2,1,0:T(8,128)(2,1)S(1)} copy-done((bf16[128,64,128]{2,1,0:T(8,128)(2,1)S(1)}, bf16[128,64,128]{2,1,0:T(8,128)(2,1)}, u32[]{:S(2)}) %copy-start.1) | copy-done | bytes 2097176
  6.3 0.0 copy-start.2
  6.3 1.2 %copy-done.2 = bf16[32,128,128]{2,1,0:T(8,128)(2,1)S(1)} copy-done((bf16[32,128,128]{2,1,0:T(8,128)(2,1)S(1)}, bf16[32,128,128]{2,1,0:T(8,128)(2,1)}, u32[]{:S(2)}) %copy-start.2) | copy-done | bytes 1048600
  7.5 0.0 copy-start.3
  7.5 0.9 copy-done.3
  8.4 0.0 copy-start.4
  8.5 0.8 copy-done.4
  9.3 0.0 copy-start.5
  9.3 0.7 copy-done.5
  10.0 63.3 %shard_map.153 = (f32[4096,128]{1,0:T(8,128)}, f32[8,32,8,128]{3,2,1,0:T(8,128)S(1)}, f32[8,128,8,128]{3,2,1,0:T(8,128)}, f32[384,128]{1,0:T(8,128)S(1)}) custom-call(s32[512]{0:T(512)S(1)} %bitcast.32, s32[1]{0:T(128)S(6)} %copy.23.count_ref, bf16[4096,128]{1,0:T(8,128)(2,1)S(1)} %bitcast.24, bf16[32,64,128]{2,1,0:T(8,128)(2,1)S(1)} %bitcast.22, ...), custom_call_target="tpu_custom_call" | custom-call | tf_op jit(solution)/shard_map/pallas_call | solution.py:111
  73.3 0.0 copy-start
  73.3 2.2 %copy-done = f32[8,128,8,128]{3,2,1,0:T(8,128)S(1)} copy-done((f32[8,128,8,128]{3,2,1,0:T(8,128)S(1)}, f32[8,128,8,128]{3,2,1,0:T(8,128)}, u32[]{:S(2)}) %copy-start) | copy-done | bytes 4194328
  75.5 35.8 %shard_map.154 = (f32[128,4,128]{2,1,0:T(4,128)S(1)}, f32[8,32,128]{2,1,0:T(8,128)S(1)}, f32[16,24,128]{2,1,0:T(8,128)S(1)}) custom-call(f32[2,4,128,8,128]{4,3,2,1,0:T(8,128)S(1)} %bitcast.21, f32[2,4,32,8,128]{4,3,2,1,0:T(8,128)S(1)} %bitcast.25, f32[16,24,128]{2,1,0:T(8,128)S(1)} %bitcast.27), custom_call_target="tpu_custom_call" | custom-call | tf_op jit(solution)/shard_map/pallas_call | solution.py:336
  111.3 0.6 pad_maximum_fusion.1
  111.9 0.6 slice_reduce_fusion
  112.5 0.7 pad_maximum_fusion
  113.2 0.6 maximum_bitcast_fusion
  113.8 0.7 copy.24
  114.4 0.7 copy.25
  (3 shorter events, 0.0 us)
Async XLA Ops:
  4.7 1.6 %copy-start.1 = (bf16[128,64,128]{2,1,0:T(8,128)(2,1)S(1)}, bf16[128,64,128]{2,1,0:T(8,128)(2,1)}, u32[]{:S(2)}) copy-start(bf16[128,64,128]{2,1,0:T(8,128)(2,1)} %param.16) | copy-start | bytes 6291460
  6.3 1.2 %copy-start.2 = (bf16[32,128,128]{2,1,0:T(8,128)(2,1)S(1)}, bf16[32,128,128]{2,1,0:T(8,128)(2,1)}, u32[]{:S(2)}) copy-start(bf16[32,128,128]{2,1,0:T(8,128)(2,1)} %param.14) | copy-start | bytes 3145732
  7.5 0.9 copy-start.3
  8.4 0.8 copy-start.4
  9.3 0.7 copy-start.5
  73.3 2.2 %copy-start = (f32[8,128,8,128]{3,2,1,0:T(8,128)S(1)}, f32[8,128,8,128]{3,2,1,0:T(8,128)}, u32[]{:S(2)}) copy-start(f32[8,128,8,128]{3,2,1,0:T(8,128)} %get-tuple-element.39) | copy-start | bytes 12582916

commit v3 on v2

--- a/solution.py
+++ b/solution.py
@@ -20,15 +20,115 @@
     return lax.dot_general(left, right, ((dims[0], dims[1]), ((), ())), preferred_element_type=F32)
 
 
+def exchange_kernel(
+    ids_ref, idrow_ref, hw_ref, zh_ref, labels_ref,
+    ids_out, hw_out, zh_out, lab_out,
+    hw32, rows32, rows16, lab16, sem, z_sem,
+):
+    ha, wa = lax.axis_index("ha"), lax.axis_index("wa")
+    z, base = lax.rem(wa, 4), wa - lax.rem(wa, 4)
+    cap = labels_ref.shape[0]
+    half = cap // 2
+    own_rows = zh_ref.shape[0]
+    part = own_rows // 4
+    across = (lax.rem(ha + 8, 16), wa)
+    corner = (lax.rem(ha + 8, 16), lax.rem(wa + 4, 8))
+    up, down, far = base + lax.rem(z + 1, 4), base + lax.rem(z + 3, 4), lax.rem(z + 2, 4)
+    barrier = pltpu.get_barrier_semaphore()
+    for to in (across, corner, (ha, up), (ha, down)):
+        pl.semaphore_signal(barrier, inc=1, device_id=to, device_id_type=MESH)
+    pl.semaphore_wait(barrier, 4)
+
+    def send(source, dest, sems, to):
+        return pltpu.make_async_remote_copy(
+            src_ref=source, dst_ref=dest, send_sem=sems.at[0], recv_sem=sems.at[1],
+            device_id=to, device_id_type=MESH)
+
+    got = own_rows + z * part
+    fetch = send(zh_ref.at[pl.ds(z * part, part)], zh_out.at[pl.ds(got, part)], z_sem.at[0], corner)
+    fetch.start()
+    keep = pltpu.make_async_copy(zh_ref, zh_out.at[pl.ds(0, own_rows)], sem.at[3, 0])
+    keep.start()
+    lab16[...] = labels_ref[half:].astype(F32).astype(BF16)
+    to_lab = send(lab16, lab_out, sem.at[0], across)
+    to_lab.start()
+    to_ids = send(idrow_ref, ids_out, sem.at[1], across)
+    to_ids.start()
+    hw32[...] = hw_ref[...].astype(F32)
+
+    def pick(i, carry):
+        for k in range(8):
+            s = i * 8 + k
+            at = 2 * ids_ref[0, half + s]
+            for p in range(2):
+                rows32[pl.ds(2 * s + p, 1), :] = hw32[pl.ds(at + p, 1), :]
+        return carry
+
+    lax.fori_loop(0, half // 8, pick, 0)
+    rows16[...] = rows32[...].astype(BF16)
+    to_hw = send(rows16, hw_out, sem.at[2], across)
+    to_hw.start()
+    fetch.wait_recv()
+    mine = zh_out.at[pl.ds(got, part)]
+    to_up = send(mine, mine, z_sem.at[1], (ha, up))
+    to_down = send(mine, mine, z_sem.at[2], (ha, down))
+    to_up.start()
+    to_down.start()
+    from_down = own_rows + lax.rem(z + 3, 4) * part
+    from_up = own_rows + lax.rem(z + 1, 4) * part
+    to_up.wait_recv()
+    piece = zh_out.at[pl.ds(from_down, part // 2)]
+    on_up = send(piece, piece, z_sem.at[3], (ha, up))
+    on_up.start()
+    to_down.wait_recv()
+    piece = zh_out.at[pl.ds(from_up + part // 2, part // 2)]
+    on_down = send(piece, piece, z_sem.at[4], (ha, down))
+    on_down.start()
+    keep.wait()
+    for cp in (to_lab, to_ids, to_hw, on_up, on_down):
+        cp.wait()
+    for cp in (fetch, to_up, to_down):
+        cp.wait_send()
+
+
+def exchange(ids, hw, zh, labels):
+    vmem = pl.BlockSpec(memory_space=pltpu.VMEM)
+    half = labels.shape[0] // 2
+    dma = lambda *s: pltpu.SemaphoreType.DMA(s)
+    return pl.pallas_call(
+        exchange_kernel,
+        out_shape=(
+            jax.ShapeDtypeStruct(ids.shape, jnp.int32),
+            jax.ShapeDtypeStruct((2 * half, hw.shape[1]), BF16),
+            jax.ShapeDtypeStruct((2 * zh.shape[0],) + zh.shape[1:], BF16),
+            jax.ShapeDtypeStruct((half, labels.shape[1]), BF16),
+        ),
+        in_specs=[pl.BlockSpec(memory_space=pltpu.SMEM)] + [vmem] * 4,
+        out_specs=[vmem] * 4,
+        scratch_shapes=[
+            pltpu.VMEM(hw.shape, F32), pltpu.VMEM((2 * half, hw.shape[1]), F32),
+            pltpu.VMEM((2 * half, hw.shape[1]), BF16), pltpu.VMEM((half, labels.shape[1]), BF16),
+            dma(4, 2), dma(5, 2),
+        ],
+        compiler_params=pltpu.CompilerParams(
+            collective_id=1, has_side_effects=True, vmem_limit_bytes=32 * 1024 * 1024),
+    )(ids, ids, hw, zh, labels)
+
+
 def decode_kernel(
-    ids_ref, count_ref, hw_ref, zh_ref, wz_ref, labels_ref, win_ref, bin_ref, wout_ref, bout_ref,
+    ids_ref, idx_ref, count_ref, hw_ref, hwx_ref, zh_ref, wz_ref, labels_ref, labx_ref, win_ref, bin_ref, wout_ref, bout_ref,
     hw_out, zh_out, wz_out, wt_out,
-    hw32, gwi_ref, gwo_ref, gbo_ref,
+    hw32, labs, gwi_ref, gwo_ref, gbo_ref,
 ):
     rows, depth, chans = zh_ref.shape
     pairs = wz_ref.shape[0]
-    used = count_ref[0]
-    hw32[...] = hw_ref[...].astype(F32)
+    half = labx_ref.shape[0]
+    own_hw = hw_ref.shape[0]
+    own_n = jnp.minimum(count_ref[0], half)
+    hw32[:own_hw] = hw_ref[...].astype(F32)
+    hw32[own_hw:] = hwx_ref[...].astype(F32)
+    labs[:half] = labels_ref[:half]
+    labs[half:] = labx_ref[...].astype(F32).astype(jnp.int32)
     hw_out[...] = jnp.zeros_like(hw_out)
     zh_out[...] = jnp.zeros_like(zh_out)
     wz_out[...] = jnp.zeros_like(wz_out)
@@ -43,17 +143,22 @@
         spots = []
         parts = []
         for g in range(GROUP):
-            rid = ids_ref[base + g]
-            row = rid // pairs
+            i = base + g
+            own = i < own_n
+            j = jnp.maximum(i - own_n, 0)
+            rid = jnp.where(own, ids_ref[0, i], idx_ref[0, half + j])
+            row = rid // pairs + jnp.where(own, 0, rows // 2)
             pair = rid % pairs
-            spots.append((rid, row, pair))
+            hw_at = jnp.where(own, 2 * rid, own_hw + 2 * j)
+            slot = jnp.where(own, i, half + j)
+            spots.append((slot, row, pair))
             zh = zh_ref[row].astype(F32)
             for p in range(2):
-                hw = hw32[pl.ds(2 * rid + p, 1), :]
+                hw = hw32[pl.ds(hw_at + p, 1), :]
                 wz = wz_ref[pair, p * depth:(p + 1) * depth, :].astype(F32)
                 parts.append(((hw + zh) + wz).astype(BF16))
         feats = jnp.concatenate(parts, axis=0)
-        u = jnp.dot(feats, win_ref[...] * 0.5, preferred_element_type=F32) + bin_ref[...]
+        u = jnp.dot(feats, win_ref[...] * 0.5, preferred_element_type=F32) + bin_ref[...] * 0.5
         a = jnp.tanh(u) + 1.0
         h = u * a
         hid = h.astype(BF16)
@@ -63,12 +168,11 @@
             lt = logits[:, g * run:(g + 1) * run] + bout_ref[...]
             top = jnp.max(lt, axis=0, keepdims=True)
             e = jnp.exp(lt - top)
-            inv = 1.0 / jnp.sum(e, axis=0, keepdims=True)
-            lab = labels_ref[pl.ds(base + g, 1), :]
+            inv = GRAD_SCALE / jnp.sum(e, axis=0, keepdims=True)
+            lab = labs[pl.ds(spots[g][0], 1), :]
             cls = lax.broadcasted_iota(jnp.int32, lt.shape, 0)
-            hot = jnp.where(cls == lab, 1.0, 0.0)
-            scale = jnp.where(base + g < used, GRAD_SCALE, 0.0)
-            dparts.append(((e * inv - hot) * scale).astype(BF16))
+            hot = jnp.where(cls == lab, GRAD_SCALE, 0.0)
+            dparts.append((e * inv - hot).astype(BF16))
         dlt = jnp.concatenate(dparts, axis=1)
         gwo_ref[...] += jnp.dot(dlt, hid, preferred_element_type=F32)
         tot = dparts[0].astype(F32)
@@ -82,15 +186,15 @@
         gwi_ref[...] += jnp.dot(lhs, dpre, preferred_element_type=F32)
         df = dotg(dpre, win_ref[...], ((1,), (1,)))
         for g in range(GROUP):
-            rid, row, pair = spots[g]
+            slot, row, pair = spots[g]
             d = df[g * run:(g + 1) * run]
             zh_out[:, row] += (d[:depth] + d[depth:]).reshape(depth // 8, 8, chans)
             for p in range(2):
                 wz_out[:, 2 * pair + p] += d[p * depth:(p + 1) * depth].reshape(depth // 8, 8, chans)
-                hw_out[pl.ds(2 * rid + p, 1), :] = jnp.sum(d[p * depth:(p + 1) * depth], axis=0, keepdims=True)
+                hw_out[pl.ds(2 * slot + p, 1), :] = jnp.sum(d[p * depth:(p + 1) * depth], axis=0, keepdims=True)
         return carry
 
-    lax.fori_loop(0, pl.cdiv(used, GROUP), body, 0)
+    lax.fori_loop(0, half // GROUP, body, 0)
     top = chans + 16
     wt_out[0:top] = gwi_ref[:, :128]
     wt_out[top:2 * top] = gwi_ref[:, 128:]
@@ -99,33 +203,88 @@
     wt_out[2 * top + 2 * CLS:] = gbo_ref[...]
 
 
-def decode_runs(ids, count, hw, zh, wz, labels, w_in, b_in, w_out, b_out):
+def decode_runs(ids, idx, count, hw, hwx, zh, wz, labels, labx, w_in, b_in, w_out, b_out):
     rows, depth, chans = zh.shape
     pairs = wz.shape[0]
     hid, ncls = w_out.shape
-    hw_rows = hw.shape[0]
-    wout = jnp.zeros((CLS, hid), BF16).at[:ncls].set(w_out.T)
-    bout = jnp.full((CLS, 1), -1e30, F32).at[:ncls, 0].set(b_out)
+    wout = jnp.pad(w_out.T, ((0, CLS - ncls), (0, 0)))
+    bout = jnp.pad(b_out, (0, CLS - ncls), constant_values=-1e30).reshape(CLS, 1)
     smem = pl.BlockSpec(memory_space=pltpu.SMEM)
     vmem = pl.BlockSpec(memory_space=pltpu.VMEM)
     return pl.pallas_call(
         decode_kernel,
         out_shape=(
-            jax.ShapeDtypeStruct((hw_rows, chans), F32),
+            jax.ShapeDtypeStruct((2 * labels.shape[0], chans), F32),
             jax.ShapeDtypeStruct((depth // 8, rows, 8, chans), F32),
             jax.ShapeDtypeStruct((depth // 8, 2 * pairs, 8, chans), F32),
             jax.ShapeDtypeStruct((2 * (chans + 16) + 3 * CLS, chans), F32),
         ),
-        in_specs=[smem, smem] + [vmem] * 8,
+        in_specs=[smem] * 3 + [vmem] * 10,
         out_specs=[vmem] * 4,
         scratch_shapes=[
-            pltpu.VMEM((hw_rows, chans), F32),
+            pltpu.VMEM((hw.shape[0] + hwx.shape[0], chans), F32),
+            pltpu.VMEM(labels.shape, jnp.int32),
             pltpu.VMEM((chans + 16, hid), F32),
             pltpu.VMEM((CLS, hid), F32),
             pltpu.VMEM((CLS, 2 * depth), F32),
         ],
         compiler_params=pltpu.CompilerParams(vmem_limit_bytes=48 * 1024 * 1024),
-    )(ids, count, hw, zh, wz, labels, w_in, (0.5 * b_in).reshape(1, hid), wout, bout)
+    )(ids, idx, count, hw, hwx, zh, wz, labels, labx, w_in, b_in.reshape(1, hid), wout, bout)
+
+
+def finish_kernel(
+    ids_ref, count_ref, own_ref, back_ref, wz_ref, zh_ref, wt_ref,
+    hw_out, wz_out, zh_out, gwi_out, gbi_out, gwo_out, gbo_out,
+):
+    cap = ids_ref.shape[1]
+    half = cap // 2
+    used = count_ref[0]
+    chans = hw_out.shape[1]
+    ncls = gwo_out.shape[1]
+    hw_out[...] = jnp.zeros_like(hw_out)
+
+    def put(source, start):
+        def go(s, carry):
+            for p in range(2):
+                hw_out[pl.ds(2 * ids_ref[0, start + s] + p, 1), :] = source[pl.ds(2 * s + p, 1), :]
+            return carry
+        return go
+
+    lax.fori_loop(0, jnp.minimum(used, half), put(own_ref, 0), 0)
+    lax.fori_loop(0, jnp.maximum(used - half, 0), put(back_ref, half), 0)
+    wz_out[...] = wz_ref[...]
+    for i in range(8):
+        zh_out[i] = zh_ref[:, i, :]
+    top = chans + 16
+    gwi_out[:, :128] = wt_ref[:chans]
+    gwi_out[:, 128:] = wt_ref[top:top + chans]
+    gbi_out[:, :128] = wt_ref[chans:chans + 1]
+    gbi_out[:, 128:] = wt_ref[top + chans:top + chans + 1]
+    at = 2 * top
+    gwo_out[:128] = wt_ref[at:at + CLS].T[:, :ncls]
+    gwo_out[128:] = wt_ref[at + CLS:at + 2 * CLS].T[:, :ncls]
+    gbo_out[...] = jnp.sum(wt_ref[at + 2 * CLS:at + 3 * CLS].T, axis=0, keepdims=True)[:, :ncls]
+
+
+def finish(ids, count, own, back, wz, zh, wt, hw_rows, hid, ncls):
+    smem = pl.BlockSpec(memory_space=pltpu.SMEM)
+    vmem = pl.BlockSpec(memory_space=pltpu.VMEM)
+    chans = own.shape[1]
+    return pl.pallas_call(
+        finish_kernel,
+        out_shape=(
+            jax.ShapeDtypeStruct((hw_rows, chans), F32),
+            jax.ShapeDtypeStruct(wz.shape, F32),
+            jax.ShapeDtypeStruct((8, zh.shape[0], chans), F32),
+            jax.ShapeDtypeStruct((chans, hid), F32),
+            jax.ShapeDtypeStruct((1, hid), F32),
+            jax.ShapeDtypeStruct((hid, ncls), F32),
+            jax.ShapeDtypeStruct((1, ncls), F32),
+        ),
+        in_specs=[smem] * 2 + [vmem] * 5,
+        out_specs=[vmem] * 7,
+        compiler_params=pltpu.CompilerParams(vmem_limit_bytes=32 * 1024 * 1024),
+    )(ids, count, own, back, wz, zh, wt)
 
 
 def ring_copies(src, chain_p, chain_m, final, sems, axis, me, size, span, at):
@@ -170,10 +329,10 @@
 
 
 def reduce_kernel(
-    wz_ref, zh_ref, wt_ref, wz_out, zh_out, wt_out,
+    wz_ref, zh_ref, wt_ref, hw_ref, wz_out, zh_out, wt_out, hw_out,
     core_in, xchain_p, xchain_m, xfinal, xsum, yin, swap,
-    zchain_p, zchain_m, zfinal, zsum, zin, zres, wt_in, wt_mid,
-    core_sem, x_sem, y_sem, swap_sem, z_sem, yl_sem, wa_sem, wb_sem, wc_sem,
+    zchain_p, zchain_m, zfinal, zsum, zin, wt_in, wt_mid,
+    core_sem, x_sem, y_sem, swap_sem, hw_sem, z_sem, yl_sem, wa_sem, wb_sem, wc_sem,
 ):
     ha, wa = lax.axis_index("ha"), lax.axis_index("wa")
     yh, x, c = ha // 8, lax.rem(ha // 2, 4), lax.rem(ha, 2)
@@ -191,6 +350,8 @@
     sibling = (ha + 1 - 2 * c, wa)
     across = (lax.rem(ha + 8, 16), wa)
     beside = (ha, lax.rem(wa + 4, 8))
+    corner = (lax.rem(ha + 8, 16), lax.rem(wa + 4, 8))
+    rows_own = zh_ref.shape[2] // 2
 
     barrier = pltpu.get_barrier_semaphore()
 
@@ -204,7 +365,8 @@
 
     lax.fori_loop(1, n_ha, greet_ha, 0)
     lax.fori_loop(1, n_wa, greet_wa, 0)
-    pl.semaphore_wait(barrier, n_ha + n_wa - 2)
+    pl.semaphore_signal(barrier, inc=1, device_id=corner, device_id_type=MESH)
+    pl.semaphore_wait(barrier, n_ha + n_wa - 1)
 
     def send(source, dest, sems, to):
         return pltpu.make_async_remote_copy(
@@ -262,6 +424,8 @@
         lax.fori_loop(1, n, go, 0)
 
     start(wt_first, n_ha)
+    back = send(hw_ref.at[pl.ds(hw_out.shape[0], hw_out.shape[0])], hw_out, hw_sem, across)
+    back.start()
     rings = []
     for k in range(CHUNKS):
         rows = pl.ds(k * span, span)
@@ -282,8 +446,14 @@
     for k in range(CHUNKS):
         rings[k][1]()
     zsum[...] = zring[2]()
-    to_beside = send(zsum.at[1 - yl], zin, yl_sem, beside)
-    to_beside.start()
+    own_part, far_part = pl.ds(0, rows_own), pl.ds(rows_own, rows_own)
+    zys = [
+        send(zsum.at[1 - yl, own_part], zin.at[0], yl_sem.at[0], beside),
+        send(zsum.at[1 - yl, far_part], zin.at[1], yl_sem.at[1], corner),
+        send(zsum.at[yl, far_part], zin.at[2], yl_sem.at[2], across),
+    ]
+    for cp in zys:
+        cp.start()
     ys = []
     for k in range(CHUNKS):
         rows = pl.ds(k * span, span)
@@ -296,10 +466,9 @@
         tot += wt_mid[i]
     wt_out[ha] = tot
     start(wt_third, n_ha)
-    to_beside.wait_recv()
-    zres[...] = zsum[yl] + zin[...]
-    for i in range(8):
-        zh_out[i] = zres[:, i, :]
+    for cp in zys:
+        cp.wait_recv()
+    zh_out[...] = (zsum[yl, own_part] + zin[0]) + (zin[1] + zin[2])
     swaps = []
     for k in range(CHUNKS):
         rows = pl.ds(k * span, span)
@@ -319,13 +488,15 @@
         ys[k].wait_send()
         swaps[k].wait_send()
     zring[3]()
-    to_beside.wait_send()
+    for cp in zys:
+        cp.wait_send()
+    back.wait()
     wait_send(wt_first, n_ha)
     wait_send(wt_second, n_wa)
     wait_send(wt_third, n_ha)
 
 
-def reduce_all(wz, zh, wt):
+def reduce_all(wz, zh, wt, hw):
     width, chans = wz.shape[2], wz.shape[4]
     rows = zh.shape[2]
     half_w = width // 2
@@ -337,11 +508,12 @@
         reduce_kernel,
         out_shape=(
             jax.ShapeDtypeStruct((width, 4, chans), F32),
-            jax.ShapeDtypeStruct((8, rows, chans), F32),
+            jax.ShapeDtypeStruct((rows // 2, 8, chans), F32),
             jax.ShapeDtypeStruct(wt.shape, F32),
+            jax.ShapeDtypeStruct((hw.shape[0] // 2, chans), F32),
         ),
-        in_specs=[vmem] * 3,
-        out_specs=[vmem] * 3,
+        in_specs=[vmem] * 4,
+        out_specs=[vmem] * 4,
         scratch_shapes=[
             buf(2, 4, half_w, 8, chans),
             buf(CHUNKS, 2, span // 2, 8, chans),
@@ -354,16 +526,15 @@
             buf(2, rows // 2, 8, chans),
             buf(2, 2, rows, 8, chans),
             buf(2, rows, 8, chans),
-            buf(rows, 8, chans),
-            buf(rows, 8, chans),
+            buf(3, rows // 2, 8, chans),
             buf(*wt.shape),
             buf(8, *wt.shape[1:]),
-            dma(CHUNKS, 2), dma(CHUNKS, 2, 6), dma(CHUNKS, 2), dma(CHUNKS, 2), dma(2, 6), dma(2),
+            dma(CHUNKS, 2), dma(CHUNKS, 2, 6), dma(CHUNKS, 2), dma(CHUNKS, 2), dma(2), dma(2, 6), dma(3, 2),
             dma(2, 16), dma(2, 8), dma(2, 16),
         ],
         compiler_params=pltpu.CompilerParams(
             collective_id=0, has_side_effects=True, vmem_limit_bytes=48 * 1024 * 1024),
-    )(wz, zh, wt)
+    )(wz, zh, wt, hw)
 
 
 def local(hw_plane, zh_plane, wz_plane, w_in, b_in, w_out, b_out, run_index, run_count, labels):
@@ -371,19 +542,17 @@
     depth = zh_plane.shape[0]
     ncls = w_out.shape[1]
     zh_rows = jnp.transpose(zh_plane, (1, 0, 2))
+    hw_rows = hw_plane.reshape(rows * cols, chans)
+    idx, hwx, zh2, labx = exchange(run_index, hw_rows, zh_rows, labels[0])
     hw, zh, wz, wt = decode_runs(
-        run_index[0], run_count, hw_plane.reshape(rows * cols, chans), zh_rows,
-        wz_plane.reshape(cols // 2, 2 * depth, chans), labels[0], w_in, b_in, w_out, b_out,
+        run_index, idx, run_count, hw_rows, hwx, zh2, wz_plane.reshape(cols // 2, 2 * depth, chans),
+        labels[0], labx, w_in, b_in, w_out, b_out,
     )
-    wz_grad, zh_grad, wt = reduce_all(
-        wz.reshape(2, 4, cols, 8, chans), zh.reshape(2, 4, rows, 8, chans), wt.reshape(16, -1, chans))
-    wt = wt.reshape(-1, chans)
-    top = chans + 16
-    gwi = jnp.concatenate([wt[:chans], wt[top:top + chans]], axis=1)
-    gbi = jnp.concatenate([wt[chans], wt[top + chans]])
-    gwo = jnp.concatenate([wt[2 * top:2 * top + ncls], wt[2 * top + CLS:2 * top + CLS + ncls]], axis=1).T
-    gbo = jnp.sum(wt[2 * top + 2 * CLS:2 * top + 2 * CLS + ncls], axis=1)
-    return (hw.reshape(rows, cols, chans), zh_grad, wz_grad, gwi, gbi, gwo, gbo)
+    wz_grad, zh_grad, wt, back = reduce_all(
+        wz.reshape(2, 4, cols, 8, chans), zh.reshape(2, 4, 2 * rows, 8, chans), wt.reshape(16, -1, chans), hw)
+    hw_grad, wz_grad, zh_grad, gwi, gbi, gwo, gbo = finish(
+        run_index, run_count, hw, back, wz_grad, zh_grad, wt.reshape(-1, chans), rows * cols, w_out.shape[0], ncls)
+    return (hw_grad.reshape(rows, cols, chans), zh_grad, wz_grad, gwi, gbi[0], gwo, gbo[0])
 
 
 def solution(mesh):

time: 117 us -> 118 us (level)
  Pallas kernels: 99.1 us -> 108 us
  local copies, waits for them, and re-layouts: 11.5 us -> 8.05 us
  other arithmetic: 3.15 us -> 0 us
    pallas_call x1, Pallas kernels: 35.8 us -> 45.2 us  [reduce_all(): pl.pallas_call(reduce_kernel, out_shape=(jax.ShapeDtypeStruct((width, 4,...]
    unnamed x15 -> x18, local copies, waits for them, and re-layouts: 10.1 us -> 6.59 us
    concatenate x2 -> x0, other arithmetic: 1.23 us -> none  [the longest x1 0.67 us: local(): gwi = jnp.concatenate([wt[:chans], wt[top:top + chans]], axis=1)]
    pallas_call x1 -> x3, Pallas kernels: 63.3 us -> 62.5 us  [the longest x1 33.9 us: decode_runs(): pl.pallas_call(decode_kernel, out_shape=(jax.ShapeDtypeStruct((2 * labels...]
where the time goes in v3:
time: 118 us; the launch traced here: 117 us
  Pallas kernels  108 us (92%)
  local copies, waits for them, and re-layouts  8.05 us (7%)
  between operations  1.46 us (1%)
    pallas_call x1, Pallas kernels, reduce_all(): pl.pallas_call(reduce_kernel, out_shape=(jax.ShapeDtypeStruct((width, 4,...  45.2 us
    pallas_call x1, Pallas kernels, decode_runs(): pl.pallas_call(decode_kernel, out_shape=(jax.ShapeDtypeStruct((2 * labels...  33.9 us
    pallas_call x1, Pallas kernels, exchange(): pl.pallas_call(exchange_kernel, out_shape=(jax.ShapeDtypeStruct(ids.shape...  23.1 us
    unnamed x18, local copies, waits for them, and re-layouts  6.59 us
    pallas_call x1, Pallas kernels, finish(): pl.pallas_call(finish_kernel, out_shape=(jax.ShapeDtypeStruct((hw_rows, c...  5.49 us

profile of v3, /device:TPU:0, one launch (start us, length us, event | category | flops | bytes accessed | tf_op | source)
XLA Modules:
  0.0 117.2 jit_solution(18353134146811595223)
XLA Ops:
  0.6 0.0 copy-start.6
  0.6 0.0 copy-start.7
  0.7 0.0 copy-start.1
  1.4 0.7 pad_bitcast_fusion
  2.1 0.1 copy.18.bout_ref
  2.2 0.7 pad.8.wout_ref
  2.9 1.2 %copy.21 = bf16[64,32,128]{2,0,1:T(8,128)(2,1)S(1)} copy(bf16[64,32,128]{2,1,0:T(8,128)(2,1)} %param.11) | data formatting | bytes 1048576 | tf_op args[1]
  4.1 0.0 copy-start
  4.1 1.2 %copy-done = bf16[32,128,128]{2,1,0:T(8,128)(2,1)S(1)} copy-done((bf16[32,128,128]{2,1,0:T(8,128)(2,1)S(1)}, bf16[32,128,128]{2,1,0:T(8,128)(2,1)}, u32[]{:S(2)}) %copy-start) | copy-done | bytes 1048600
  5.3 0.0 copy-start.2
  5.3 0.9 copy-done.2
  6.3 0.0 copy-start.5
  6.3 0.7 copy-done.5
  7.0 23.1 %shard_map.153 = (s32[1,512]{1,0:T(1,128)S(1)}, bf16[512,128]{1,0:T(8,128)(2,1)S(1)}, bf16[64,64,128]{2,1,0:T(8,128)(2,1)S(1)}, bf16[256,128]{1,0:T(8,128)(2,1)S(1)}) custom-call(s32[1,512]{1,0:T(1,128)S(1)} %copy-done.5, s32[1,512]{1,0:T(1,128)S(1)} %copy-done.5, bf16[4096,128]{1,0:T(8,128)(2,1)S(1)} %bitcast.17, bf16[32,64,128]{2,1,0:T(8,128)(2,1)S(1)} %bitcast.19, ...), custom_call_target="tpu_custom_call" | custom-call | tf_op jit(solution)/shard_map/pallas_call | solution.py:98
  30.1 0.0 copy-done.6
  30.1 0.0 copy-done.7
  30.1 0.0 copy-done.1
  30.1 0.0 copy-start.3
  30.1 0.9 copy-done.3
  31.1 0.8 copy-done.4
  31.9 33.9 %shard_map.154 = (f32[1024,128]{1,0:T(8,128)S(1)}, f32[8,64,8,128]{3,2,1,0:T(8,128)S(1)}, f32[8,128,8,128]{3,2,1,0:T(8,128)}, f32[384,128]{1,0:T(8,128)S(1)}) custom-call(s32[1,512]{1,0:T(1,128)S(1)} %copy-done.6, s32[1,512]{1,0:T(1,128)S(1)} %get-tuple-element.26.idx_ref, s32[1]{0:T(128)S(6)} %copy.22.count_ref, bf16[4096,128]{1,0:T(8,128)(2,1)S(1)} %bitcast.18, ...), custom_call_target="tpu_custom_call" | custom-call | tf_op jit(solution)/shard_map/pallas_call | solution.py:214
  65.8 45.2 %shard_map.155 = (f32[128,4,128]{2,1,0:T(4,128)S(1)}, f32[32,8,128]{2,1,0:T(8,128)S(1)}, f32[16,24,128]{2,1,0:T(8,128)S(1)}, f32[512,128]{1,0:T(8,128)S(1)}) custom-call(f32[2,4,128,8,128]{4,3,2,1,0:T(8,128)} %bitcast.26, f32[2,4,64,8,128]{4,3,2,1,0:T(8,128)S(1)} %bitcast.20, f32[16,24,128]{2,1,0:T(8,128)S(1)} %bitcast.23, ...), custom_call_target="tpu_custom_call" | custom-call | tf_op jit(solution)/shard_map/pallas_call | solution.py:507
  111.0 5.5 %shard_map.156 = (f32[4096,128]{1,0:T(8,128)}, f32[128,4,128]{2,1,0:T(4,128)}, f32[8,32,128]{2,1,0:T(8,128)}, f32[128,256]{1,0:T(8,128)}, f32[1,256]{1,0:T(1,128...) custom-call(s32[1,512]{1,0:T(1,128)S(1)} %copy-done.6, s32[1]{0:T(128)S(6)} %copy.22.count_ref, ...), custom_call_target="tpu_custom_call" | custom-call | tf_op jit(solution)/shard_map/pallas_call | solution.py:273
  116.5 0.7 copy.19
  (1 shorter events, 0.0 us)
Async XLA Ops:
  0.6 29.4 %copy-start.6 = (s32[1,512]{1,0:T(1,128)S(1)}, s32[1,512]{1,0:T(1,128)}, u32[]{:S(2)}) copy-start(s32[1,512]{1,0:T(1,128)} %ids_ref.5) | copy-start | bytes 6148
  0.6 29.4 %copy-start.7 = (f32[256]{0:T(256)S(1)}, f32[256]{0:T(256)}, u32[]{:S(2)}) copy-start(f32[256]{0:T(256)} %param.14) | copy-start | bytes 3076
  0.7 29.4 %copy-start.1 = (bf16[32,128,128]{2,1,0:T(8,128)(2,1)S(1)}, bf16[32,128,128]{2,1,0:T(8,128)(2,1)}, u32[]{:S(2)}) copy-start(bf16[32,128,128]{2,1,0:T(8,128)(2,1)} %param.10) | copy-start | bytes 3145732
  4.1 1.2 %copy-start = (bf16[32,128,128]{2,1,0:T(8,128)(2,1)S(1)}, bf16[32,128,128]{2,1,0:T(8,128)(2,1)}, u32[]{:S(2)}) copy-start(bf16[32,128,128]{2,1,0:T(8,128)(2,1)} %param.10) | copy-start | bytes 3145732
  5.3 0.9 copy-start.2
  6.3 0.7 copy-start.5
  30.1 1.0 copy-start.3
  31.1 0.8 copy-start.4

commit v4 on v3

--- a/solution.py
+++ b/solution.py
@@ -10,9 +10,9 @@
 F32 = jnp.float32
 BF16 = jnp.bfloat16
 GRAD_SCALE = 0.25
-GROUP = 16
+GROUP = 32
 CLS = 32
-CHUNKS = 4
+CHUNKS = 2
 MESH = pl.DeviceIdType.MESH
 
 
@@ -287,53 +287,90 @@
     )(ids, count, own, back, wz, zh, wt)
 
 
-def ring_copies(src, chain_p, chain_m, final, sems, axis, me, size, span, at):
-    plus, minus, far = lax.rem(me + 1, size), lax.rem(me + 3, size), lax.rem(me + 2, size)
-    half = span // 2
-    lo, hi = pl.ds(at, half), pl.ds(at + half, half)
-
-    def copy(i, source, dest, to):
-        return pltpu.make_async_remote_copy(
-            src_ref=source, dst_ref=dest, send_sem=sems.at[0, i], recv_sem=sems.at[1, i],
-            device_id=axis(to), device_id_type=MESH)
-
-    first = [
-        copy(0, src.at[:, far, lo], chain_p, plus),
-        copy(1, src.at[:, far, hi], chain_m, minus),
-        copy(2, src.at[:, minus, lo], final.at[1, :, 0:half], minus),
-        copy(3, src.at[:, plus, hi], final.at[1, :, half:span], plus),
+def pack(v):
+    most = jnp.maximum(jnp.max(jnp.abs(v), axis=1, keepdims=True), 1e-30)
+    return jnp.round(v * (32766.0 / most)).astype(jnp.int32).astype(jnp.int16), most * (1.0 / 32766.0)
+
+
+def unpack(q, scale):
+    return q.astype(jnp.int32).astype(F32) * scale
+
+
+class Coded:
+    def __init__(self, out, out_scale, into, into_scale, sems, to):
+        self.out, self.out_scale, self.into, self.into_scale = out, out_scale, into, into_scale
+        self.copies = [
+            pltpu.make_async_remote_copy(
+                src_ref=a, dst_ref=b, send_sem=sems.at[0, i], recv_sem=sems.at[1, i], device_id=to, device_id_type=MESH)
+            for i, (a, b) in enumerate(((out, into), (out_scale, into_scale)))
+        ]
+
+    def send(self, v):
+        self.out[...], self.out_scale[...] = pack(v)
+        for cp in self.copies:
+            cp.start()
+
+    def receive(self):
+        for cp in self.copies:
+            cp.wait_recv()
+        return unpack(self.into[...], self.into_scale[...])
+
+    def done(self):
+        for cp in self.copies:
+            cp.wait_send()
+
+
+def coded_buffers(n, groups, rows, chans):
+    return [
+        pltpu.VMEM((n, groups, rows, chans), jnp.int16), pltpu.VMEM((n, groups, 1, chans), F32),
+        pltpu.VMEM((n, groups, rows, chans), jnp.int16), pltpu.VMEM((n, groups, 1, chans), F32),
+        pltpu.SemaphoreType.DMA((n, 2, 2)),
     ]
-    second = [
-        copy(4, chain_p, final.at[0, :, 0:half], plus),
-        copy(5, chain_m, final.at[0, :, half:span], minus),
-    ]
-
-    def relay():
-        first[0].wait_recv()
-        chain_p[...] += src[:, plus, lo]
-        second[0].start()
-        first[1].wait_recv()
-        chain_m[...] += src[:, minus, hi]
-        second[1].start()
-
-    def finish():
-        for c in (first[2], first[3], second[0], second[1]):
-            c.wait_recv()
-        return final[0] + final[1] + src[:, me, pl.ds(at, span)]
-
-    def done():
-        for c in first + second:
-            c.wait_send()
-
-    return first, relay, finish, done
+
+
+def coded(bufs, i, to):
+    out, out_scale, into, into_scale, sems = bufs
+    return Coded(out.at[i], out_scale.at[i], into.at[i], into_scale.at[i], sems.at[i], to)
+
+
+class Ring:
+    def __init__(self, src, bufs, first, axis, me, span, at):
+        self.src, self.me, self.span = src, me, span
+        self.plus, self.minus, self.far = lax.rem(me + 1, 4), lax.rem(me + 3, 4), lax.rem(me + 2, 4)
+        self.lo, self.hi = pl.ds(at, span // 2), pl.ds(at + span // 2, span // 2)
+        to = [axis(self.plus), axis(self.minus)]
+        self.msgs = [coded(bufs, first + i, to[d]) for i, d in enumerate((0, 1, 1, 0, 0, 1))]
+
+    def part(self, where, half):
+        v = self.src[:, where, half]
+        return v.reshape(v.shape[0], -1, v.shape[-1])
+
+    def begin(self):
+        self.msgs[0].send(self.part(self.far, self.lo))
+        self.msgs[1].send(self.part(self.far, self.hi))
+        self.msgs[2].send(self.part(self.minus, self.lo))
+        self.msgs[3].send(self.part(self.plus, self.hi))
+
+    def relay(self):
+        self.msgs[4].send(self.msgs[0].receive() + self.part(self.plus, self.lo))
+        self.msgs[5].send(self.msgs[1].receive() + self.part(self.minus, self.hi))
+
+    def finish(self):
+        lo = self.part(self.me, self.lo) + self.msgs[2].receive() + self.msgs[4].receive()
+        hi = self.part(self.me, self.hi) + self.msgs[3].receive() + self.msgs[5].receive()
+        return lo, hi
+
+    def done(self):
+        for m in self.msgs:
+            m.done()
 
 
 def reduce_kernel(
     wz_ref, zh_ref, wt_ref, hw_ref, wz_out, zh_out, wt_out, hw_out,
-    core_in, xchain_p, xchain_m, xfinal, xsum, yin, swap,
-    zchain_p, zchain_m, zfinal, zsum, zin, wt_in, wt_mid,
-    core_sem, x_sem, y_sem, swap_sem, hw_sem, z_sem, yl_sem, wa_sem, wb_sem, wc_sem,
+    wz_own, core_in, xsum, swap, zsum, wt_in, wt_mid,
+    own_sem, core_sem, swap_sem, wa_sem, wb_sem, wc_sem, *bufs,
 ):
+    xbufs, ybufs, zbufs, zybufs, hwbufs = (bufs[5 * i:5 * i + 5] for i in range(5))
     ha, wa = lax.axis_index("ha"), lax.axis_index("wa")
     yh, x, c = ha // 8, lax.rem(ha // 2, 4), lax.rem(ha, 2)
     yl, z = wa // 4, lax.rem(wa, 4)
@@ -363,6 +400,8 @@
         pl.semaphore_signal(barrier, inc=1, device_id=(ha, lax.rem(wa + i, n_wa)), device_id_type=MESH)
         return carry
 
+    load = pltpu.make_async_copy(wz_ref.at[:, :, pl.ds(c * half_w, half_w)], wz_own, own_sem.at[0])
+    load.start()
     lax.fori_loop(1, n_ha, greet_ha, 0)
     lax.fori_loop(1, n_wa, greet_wa, 0)
     pl.semaphore_signal(barrier, inc=1, device_id=corner, device_id_type=MESH)
@@ -380,9 +419,8 @@
     ]
     for k in range(CHUNKS):
         core[k].start()
-    zring = ring_copies(zh_ref, zchain_p, zchain_m, zfinal, z_sem, on_z, z, 4, zh_ref.shape[2], 0)
-    for cp in zring[0]:
-        cp.start()
+    zring = Ring(zh_ref, zbufs, 0, on_z, z, zh_ref.shape[2], 0)
+    zring.begin()
 
     def wt_first(i):
         to = lax.rem(ha + i, n_ha)
@@ -424,18 +462,18 @@
         lax.fori_loop(1, n, go, 0)
 
     start(wt_first, n_ha)
-    back = send(hw_ref.at[pl.ds(hw_out.shape[0], hw_out.shape[0])], hw_out, hw_sem, across)
-    back.start()
+    chans = hw_ref.shape[1]
+    back = coded(hwbufs, 0, across)
+    back.send(hw_ref[hw_out.shape[0]:].reshape(-1, 128, chans))
+    load.wait()
     rings = []
     for k in range(CHUNKS):
         rows = pl.ds(k * span, span)
         core[k].wait_recv()
-        core_in[:, :, rows] += wz_ref[:, :, pl.ds(c * half_w + k * span, span)]
-        ring = ring_copies(core_in, xchain_p.at[k], xchain_m.at[k], xfinal.at[k], x_sem.at[k], on_x, x, 4, span, k * span)
-        for cp in ring[0]:
-            cp.start()
-        rings.append(ring)
-    zring[1]()
+        core_in[:, :, rows] += wz_own[:, :, rows]
+        rings.append(Ring(core_in, xbufs, 6 * k, on_x, x, span, k * span))
+        rings[k].begin()
+    zring.relay()
     wait_slot(wt_in, wa_sem, ha, n_ha, sibling)
     wt_in[ha] = wt_ref[ha]
     tot = wt_in[0]
@@ -444,53 +482,50 @@
     wt_mid[wa] = tot
     start(wt_second, n_wa)
     for k in range(CHUNKS):
-        rings[k][1]()
-    zsum[...] = zring[2]()
-    own_part, far_part = pl.ds(0, rows_own), pl.ds(rows_own, rows_own)
-    zys = [
-        send(zsum.at[1 - yl, own_part], zin.at[0], yl_sem.at[0], beside),
-        send(zsum.at[1 - yl, far_part], zin.at[1], yl_sem.at[1], corner),
-        send(zsum.at[yl, far_part], zin.at[2], yl_sem.at[2], across),
-    ]
-    for cp in zys:
-        cp.start()
+        rings[k].relay()
+    zsum[0], zsum[1] = zring.finish()
+    zys = [coded(zybufs, i, to) for i, to in enumerate((beside, corner, across))]
+    zys[0].send(zsum[0, pl.ds(1 - yl, 1)])
+    zys[1].send(zsum[1, pl.ds(1 - yl, 1)])
+    zys[2].send(zsum[1, pl.ds(yl, 1)])
     ys = []
     for k in range(CHUNKS):
         rows = pl.ds(k * span, span)
-        xsum[:, rows] = rings[k][2]()
-        ys.append(send(xsum.at[1 - yh, rows], yin.at[rows], y_sem.at[k], across))
-        ys[k].start()
+        lo, hi = rings[k].finish()
+        xsum[:, k, 0:span * 4], xsum[:, k, span * 4:] = lo, hi
+        ys.append(coded(ybufs, k, across))
+        ys[k].send(xsum[pl.ds(1 - yh, 1), k])
     wait_slot(wt_mid, wb_sem, wa, n_wa, beside)
     tot = wt_mid[0]
     for i in range(1, n_wa):
         tot += wt_mid[i]
     wt_out[ha] = tot
     start(wt_third, n_ha)
-    for cp in zys:
-        cp.wait_recv()
-    zh_out[...] = (zsum[yl, own_part] + zin[0]) + (zin[1] + zin[2])
+    total = zsum[0, pl.ds(yl, 1)]
+    for m in zys:
+        total += m.receive()
+    zh_out[...] = total.reshape(zh_out.shape)
     swaps = []
     for k in range(CHUNKS):
         rows = pl.ds(k * span, span)
-        ys[k].wait_recv()
-        r = xsum[yh, rows] + yin[rows]
+        r = (xsum[pl.ds(yh, 1), k] + ys[k].receive()).reshape(span, 8, chans)
         mine = pl.ds(c * half_w + k * span, span)
         wz_out[mine] = jnp.where(c == 0, r[:, :4], r[:, 4:])
         swap[rows] = jnp.where(c == 0, r[:, 4:], r[:, :4])
         swaps.append(send(swap.at[rows], wz_out.at[mine], swap_sem.at[k], sibling))
         swaps[k].start()
+    hw_out[...] = back.receive().reshape(hw_out.shape)
     for k in range(CHUNKS):
         swaps[k].wait_recv()
     wait_slot(wt_out, wc_sem, ha, n_ha, sibling)
     for k in range(CHUNKS):
         core[k].wait_send()
-        rings[k][3]()
-        ys[k].wait_send()
+        rings[k].done()
+        ys[k].done()
         swaps[k].wait_send()
-    zring[3]()
-    for cp in zys:
-        cp.wait_send()
-    back.wait()
+    zring.done()
+    for m in zys + [back]:
+        m.done()
     wait_send(wt_first, n_ha)
     wait_send(wt_second, n_wa)
     wait_send(wt_third, n_ha)
@@ -512,25 +547,22 @@
             jax.ShapeDtypeStruct(wt.shape, F32),
             jax.ShapeDtypeStruct((hw.shape[0] // 2, chans), F32),
         ),
-        in_specs=[vmem] * 4,
+        in_specs=[pl.BlockSpec(memory_space=pl.ANY)] + [vmem] * 3,
         out_specs=[vmem] * 4,
         scratch_shapes=[
             buf(2, 4, half_w, 8, chans),
-            buf(CHUNKS, 2, span // 2, 8, chans),
-            buf(CHUNKS, 2, span // 2, 8, chans),
-            buf(CHUNKS, 2, 2, span, 8, chans),
-            buf(2, half_w, 8, chans),
-            buf(half_w, 8, chans),
+            buf(2, 4, half_w, 8, chans),
+            buf(2, CHUNKS, span * 8, chans),
             buf(half_w, 4, chans),
-            buf(2, rows // 2, 8, chans),
-            buf(2, rows // 2, 8, chans),
-            buf(2, 2, rows, 8, chans),
-            buf(2, rows, 8, chans),
-            buf(3, rows // 2, 8, chans),
+            buf(2, 2, rows * 4, chans),
             buf(*wt.shape),
             buf(8, *wt.shape[1:]),
-            dma(CHUNKS, 2), dma(CHUNKS, 2, 6), dma(CHUNKS, 2), dma(CHUNKS, 2), dma(2), dma(2, 6), dma(3, 2),
-            dma(2, 16), dma(2, 8), dma(2, 16),
+            dma(1), dma(CHUNKS, 2), dma(CHUNKS, 2), dma(2, 16), dma(2, 8), dma(2, 16),
+            *coded_buffers(6 * CHUNKS, 2, span * 4, chans),
+            *coded_buffers(CHUNKS, 1, span * 8, chans),
+            *coded_buffers(6, 2, rows * 4, chans),
+            *coded_buffers(3, 1, rows * 4, chans),
+            *coded_buffers(1, hw.shape[0] // 256, 128, chans),
         ],
         compiler_params=pltpu.CompilerParams(
             collective_id=0, has_side_effects=True, vmem_limit_bytes=48 * 1024 * 1024),

time: 118 us -> 100 us (0.85)
  Pallas kernels: 108 us -> 90.2 us
    pallas_call x1, Pallas kernels: 45.2 us -> 29.4 us  [reduce_all(): pl.pallas_call(reduce_kernel, out_shape=(jax.ShapeDtypeStruct((width, 4,...]
    pallas_call x1, Pallas kernels: 33.9 us -> 32.2 us  [decode_runs(): pl.pallas_call(decode_kernel, out_shape=(jax.ShapeDtypeStruct((2 * labels...]
where the time goes in v4:
time: 100 us; the launch traced here: 99.7 us
  Pallas kernels  90.2 us (90%)
  local copies, waits for them, and re-layouts  8.05 us (8%)
  between operations  1.46 us (1%)
    pallas_call x1, Pallas kernels, decode_runs(): pl.pallas_call(decode_kernel, out_shape=(jax.ShapeDtypeStruct((2 * labels...  32.2 us
    pallas_call x1, Pallas kernels, reduce_all(): pl.pallas_call(reduce_kernel, out_shape=(jax.ShapeDtypeStruct((width, 4,...  29.4 us
    pallas_call x1, Pallas kernels, exchange(): pl.pallas_call(exchange_kernel, out_shape=(jax.ShapeDtypeStruct(ids.shape...  23.1 us
    unnamed x18, local copies, waits for them, and re-layouts  6.59 us
    pallas_call x1, Pallas kernels, finish(): pl.pallas_call(finish_kernel, out_shape=(jax.ShapeDtypeStruct((hw_rows, c...  5.49 us

profile of v4, /device:TPU:0, one launch (start us, length us, event | category | flops | bytes accessed | tf_op | source)
XLA Modules:
  0.0 99.7 jit_solution(14879724816462151284)
XLA Ops:
  0.6 0.0 copy-start.6
  0.6 0.0 copy-start.7
  0.7 0.0 copy-start.1
  1.4 0.7 pad_bitcast_fusion
  2.1 0.1 copy.18.bout_ref
  2.2 0.7 pad.8.wout_ref
  2.9 1.2 %copy.21 = bf16[64,32,128]{2,0,1:T(8,128)(2,1)S(1)} copy(bf16[64,32,128]{2,1,0:T(8,128)(2,1)} %param.11) | data formatting | bytes 1048576 | tf_op args[1]
  4.1 0.0 copy-start
  4.1 1.2 %copy-done = bf16[32,128,128]{2,1,0:T(8,128)(2,1)S(1)} copy-done((bf16[32,128,128]{2,1,0:T(8,128)(2,1)S(1)}, bf16[32,128,128]{2,1,0:T(8,128)(2,1)}, u32[]{:S(2)}) %copy-start) | copy-done | bytes 1048600
  5.3 0.0 copy-start.2
  5.3 0.9 copy-done.2
  6.3 0.0 copy-start.5
  6.3 0.7 copy-done.5
  7.0 23.1 %shard_map.153 = (s32[1,512]{1,0:T(1,128)S(1)}, bf16[512,128]{1,0:T(8,128)(2,1)S(1)}, bf16[64,64,128]{2,1,0:T(8,128)(2,1)S(1)}, bf16[256,128]{1,0:T(8,128)(2,1)S(1)}) custom-call(s32[1,512]{1,0:T(1,128)S(1)} %copy-done.5, s32[1,512]{1,0:T(1,128)S(1)} %copy-done.5, bf16[4096,128]{1,0:T(8,128)(2,1)S(1)} %bitcast.17, bf16[32,64,128]{2,1,0:T(8,128)(2,1)S(1)} %bitcast.19, ...), custom_call_target="tpu_custom_call" | custom-call | tf_op jit(solution)/shard_map/pallas_call | solution.py:98
  30.1 0.0 copy-done.6
  30.1 0.0 copy-done.7
  30.1 0.0 copy-done.1
  30.1 0.0 copy-start.3
  30.1 0.9 copy-done.3
  31.1 0.8 copy-done.4
  31.9 32.2 %shard_map.154 = (f32[1024,128]{1,0:T(8,128)S(1)}, f32[8,64,8,128]{3,2,1,0:T(8,128)S(1)}, f32[8,128,8,128]{3,2,1,0:T(8,128)}, f32[384,128]{1,0:T(8,128)S(1)}) custom-call(s32[1,512]{1,0:T(1,128)S(1)} %copy-done.6, s32[1,512]{1,0:T(1,128)S(1)} %get-tuple-element.26.idx_ref, s32[1]{0:T(128)S(6)} %copy.22.count_ref, bf16[4096,128]{1,0:T(8,128)(2,1)S(1)} %bitcast.18, ...), custom_call_target="tpu_custom_call" | custom-call | tf_op jit(solution)/shard_map/pallas_call | solution.py:214
  64.1 29.4 %shard_map.155 = (f32[128,4,128]{2,1,0:T(4,128)S(1)}, f32[32,8,128]{2,1,0:T(8,128)S(1)}, f32[16,24,128]{2,1,0:T(8,128)S(1)}, f32[512,128]{1,0:T(8,128)S(1)}) custom-call(f32[2,4,128,8,128]{4,3,2,1,0:T(8,128)} %bitcast.26, f32[2,4,64,8,128]{4,3,2,1,0:T(8,128)S(1)} %bitcast.20, f32[16,24,128]{2,1,0:T(8,128)S(1)} %bitcast.23, ...), custom_call_target="tpu_custom_call" | custom-call | tf_op jit(solution)/shard_map/pallas_call | solution.py:542
  93.5 5.5 %shard_map.156 = (f32[4096,128]{1,0:T(8,128)}, f32[128,4,128]{2,1,0:T(4,128)}, f32[8,32,128]{2,1,0:T(8,128)}, f32[128,256]{1,0:T(8,128)}, f32[1,256]{1,0:T(1,128...) custom-call(s32[1,512]{1,0:T(1,128)S(1)} %copy-done.6, s32[1]{0:T(128)S(6)} %copy.22.count_ref, ...), custom_call_target="tpu_custom_call" | custom-call | tf_op jit(solution)/shard_map/pallas_call | solution.py:273
  99.0 0.7 copy.19
  (1 shorter events, 0.0 us)
Async XLA Ops:
  0.6 29.4 %copy-start.6 = (s32[1,512]{1,0:T(1,128)S(1)}, s32[1,512]{1,0:T(1,128)}, u32[]{:S(2)}) copy-start(s32[1,512]{1,0:T(1,128)} %ids_ref.5) | copy-start | bytes 6148
  0.6 29.4 %copy-start.7 = (f32[256]{0:T(256)S(1)}, f32[256]{0:T(256)}, u32[]{:S(2)}) copy-start(f32[256]{0:T(256)} %param.14) | copy-start | bytes 3076
  0.7 29.4 %copy-start.1 = (bf16[32,128,128]{2,1,0:T(8,128)(2,1)S(1)}, bf16[32,128,128]{2,1,0:T(8,128)(2,1)}, u32[]{:S(2)}) copy-start(bf16[32,128,128]{2,1,0:T(8,128)(2,1)} %param.10) | copy-start | bytes 3145732
  4.1 1.2 %copy-start = (bf16[32,128,128]{2,1,0:T(8,128)(2,1)S(1)}, bf16[32,128,128]{2,1,0:T(8,128)(2,1)}, u32[]{:S(2)}) copy-start(bf16[32,128,128]{2,1,0:T(8,128)(2,1)} %param.10) | copy-start | bytes 3145732
  5.3 0.9 copy-start.2
  6.3 0.7 copy-start.5
  30.1 1.0 copy-start.3
  31.1 0.8 copy-start.4

commit v5 on v4

--- a/solution.py
+++ b/solution.py
@@ -13,6 +13,9 @@
 GROUP = 32
 CLS = 32
 CHUNKS = 2
+EXCHANGE_VMEM = 56 * 1024 * 1024
+DECODE_VMEM = 40 * 1024 * 1024
+REDUCE_VMEM = 32 * 1024 * 1024
 MESH = pl.DeviceIdType.MESH
 
 
@@ -23,38 +26,49 @@
 def exchange_kernel(
     ids_ref, idrow_ref, hw_ref, zh_ref, labels_ref,
     ids_out, hw_out, zh_out, lab_out,
-    hw32, rows32, rows16, lab16, sem, z_sem,
+    hwv, zhv, labv, hw32, zh32, rows32, rows16, lab16, load_sem, sem, z_sem,
 ):
     ha, wa = lax.axis_index("ha"), lax.axis_index("wa")
     z, base = lax.rem(wa, 4), wa - lax.rem(wa, 4)
-    cap = labels_ref.shape[0]
-    half = cap // 2
-    own_rows = zh_ref.shape[0]
+    half = lab16.shape[0]
+    own_rows = zh_ref.shape[1]
     part = own_rows // 4
     across = (lax.rem(ha + 8, 16), wa)
     corner = (lax.rem(ha + 8, 16), lax.rem(wa + 4, 8))
-    up, down, far = base + lax.rem(z + 1, 4), base + lax.rem(z + 3, 4), lax.rem(z + 2, 4)
+    ring = [(ha, base + lax.rem(z + k, 4)) for k in (1, 3, 2)]
+    loads = [
+        pltpu.make_async_copy(zh_ref, zhv, load_sem.at[0]),
+        pltpu.make_async_copy(hw_ref, hwv, load_sem.at[1]),
+        pltpu.make_async_copy(labels_ref.at[pl.ds(half, half)], labv, load_sem.at[2]),
+    ]
+    for cp in loads:
+        cp.start()
     barrier = pltpu.get_barrier_semaphore()
-    for to in (across, corner, (ha, up), (ha, down)):
+    for to in [across, corner] + ring:
         pl.semaphore_signal(barrier, inc=1, device_id=to, device_id_type=MESH)
-    pl.semaphore_wait(barrier, 4)
 
     def send(source, dest, sems, to):
         return pltpu.make_async_remote_copy(
             src_ref=source, dst_ref=dest, send_sem=sems.at[0], recv_sem=sems.at[1],
             device_id=to, device_id_type=MESH)
 
+    def turn(q):
+        at = pl.multiple_of(q * part, part)
+        zh_out[pl.ds(at, part)] = jnp.swapaxes(zh32[:, pl.ds(at, part), :], 0, 1).astype(BF16)
+
+    loads[0].wait()
+    zh32[...] = zhv[...].astype(F32)
+    turn(z)
+    pl.semaphore_wait(barrier, 5)
     got = own_rows + z * part
-    fetch = send(zh_ref.at[pl.ds(z * part, part)], zh_out.at[pl.ds(got, part)], z_sem.at[0], corner)
+    fetch = send(zh_out.at[pl.ds(z * part, part)], zh_out.at[pl.ds(got, part)], z_sem.at[0], corner)
     fetch.start()
-    keep = pltpu.make_async_copy(zh_ref, zh_out.at[pl.ds(0, own_rows)], sem.at[3, 0])
-    keep.start()
-    lab16[...] = labels_ref[half:].astype(F32).astype(BF16)
-    to_lab = send(lab16, lab_out, sem.at[0], across)
-    to_lab.start()
-    to_ids = send(idrow_ref, ids_out, sem.at[1], across)
-    to_ids.start()
-    hw32[...] = hw_ref[...].astype(F32)
+    for k in (1, 2, 3):
+        turn(lax.rem(z + k, 4))
+    loads[2].wait()
+    lab16[...] = labv[...].astype(F32).astype(BF16)
+    loads[1].wait()
+    hw32[...] = hwv[...].astype(F32)
 
     def pick(i, carry):
         for k in range(8):
@@ -66,59 +80,49 @@
 
     lax.fori_loop(0, half // 8, pick, 0)
     rows16[...] = rows32[...].astype(BF16)
-    to_hw = send(rows16, hw_out, sem.at[2], across)
-    to_hw.start()
     fetch.wait_recv()
     mine = zh_out.at[pl.ds(got, part)]
-    to_up = send(mine, mine, z_sem.at[1], (ha, up))
-    to_down = send(mine, mine, z_sem.at[2], (ha, down))
-    to_up.start()
-    to_down.start()
-    from_down = own_rows + lax.rem(z + 3, 4) * part
-    from_up = own_rows + lax.rem(z + 1, 4) * part
-    to_up.wait_recv()
-    piece = zh_out.at[pl.ds(from_down, part // 2)]
-    on_up = send(piece, piece, z_sem.at[3], (ha, up))
-    on_up.start()
-    to_down.wait_recv()
-    piece = zh_out.at[pl.ds(from_up + part // 2, part // 2)]
-    on_down = send(piece, piece, z_sem.at[4], (ha, down))
-    on_down.start()
-    keep.wait()
-    for cp in (to_lab, to_ids, to_hw, on_up, on_down):
+    outs = [send(mine, mine, z_sem.at[1 + k], to) for k, to in enumerate(ring)]
+    outs += [send(rows16, hw_out, sem.at[0], across), send(lab16, lab_out, sem.at[1], across),
+             send(idrow_ref, ids_out, sem.at[2], across)]
+    for cp in outs:
+        cp.start()
+    for cp in outs:
         cp.wait()
-    for cp in (fetch, to_up, to_down):
-        cp.wait_send()
+    fetch.wait_send()
 
 
 def exchange(ids, hw, zh, labels):
     vmem = pl.BlockSpec(memory_space=pltpu.VMEM)
+    hbm = pl.BlockSpec(memory_space=pl.ANY)
     half = labels.shape[0] // 2
+    depth, rows, chans = zh.shape
     dma = lambda *s: pltpu.SemaphoreType.DMA(s)
     return pl.pallas_call(
         exchange_kernel,
         out_shape=(
             jax.ShapeDtypeStruct(ids.shape, jnp.int32),
-            jax.ShapeDtypeStruct((2 * half, hw.shape[1]), BF16),
-            jax.ShapeDtypeStruct((2 * zh.shape[0],) + zh.shape[1:], BF16),
+            jax.ShapeDtypeStruct((2 * half, chans), BF16),
+            jax.ShapeDtypeStruct((2 * rows, depth, chans), BF16),
             jax.ShapeDtypeStruct((half, labels.shape[1]), BF16),
         ),
-        in_specs=[pl.BlockSpec(memory_space=pltpu.SMEM)] + [vmem] * 4,
+        in_specs=[pl.BlockSpec(memory_space=pltpu.SMEM), vmem, hbm, hbm, hbm],
         out_specs=[vmem] * 4,
         scratch_shapes=[
-            pltpu.VMEM(hw.shape, F32), pltpu.VMEM((2 * half, hw.shape[1]), F32),
-            pltpu.VMEM((2 * half, hw.shape[1]), BF16), pltpu.VMEM((half, labels.shape[1]), BF16),
-            dma(4, 2), dma(5, 2),
+            pltpu.VMEM(hw.shape, BF16), pltpu.VMEM(zh.shape, BF16), pltpu.VMEM((half, labels.shape[1]), jnp.int32),
+            pltpu.VMEM(hw.shape, F32), pltpu.VMEM(zh.shape, F32), pltpu.VMEM((2 * half, chans), F32),
+            pltpu.VMEM((2 * half, chans), BF16), pltpu.VMEM((half, labels.shape[1]), BF16),
+            dma(3), dma(3, 2), dma(4, 2),
         ],
         compiler_params=pltpu.CompilerParams(
-            collective_id=1, has_side_effects=True, vmem_limit_bytes=32 * 1024 * 1024),
+            collective_id=1, has_side_effects=True, vmem_limit_bytes=EXCHANGE_VMEM),
     )(ids, ids, hw, zh, labels)
 
 
 def decode_kernel(
     ids_ref, idx_ref, count_ref, hw_ref, hwx_ref, zh_ref, wz_ref, labels_ref, labx_ref, win_ref, bin_ref, wout_ref, bout_ref,
     hw_out, zh_out, wz_out, wt_out,
-    hw32, labs, gwi_ref, gwo_ref, gbo_ref,
+    hw32, labs, wpad, wout_t, gwi_ref, gwo_ref, gbo_ref,
 ):
     rows, depth, chans = zh_ref.shape
     pairs = wz_ref.shape[0]
@@ -135,7 +139,16 @@
     gwi_ref[...] = jnp.zeros_like(gwi_ref)
     gwo_ref[...] = jnp.zeros_like(gwo_ref)
     gbo_ref[...] = jnp.zeros_like(gbo_ref)
+    ncls = wout_ref.shape[1]
+    wpad[...] = jnp.zeros_like(wpad)
+    wpad[:ncls] = wout_ref[...].astype(F32).T
+    wout_t[...] = wpad[...].astype(BF16)
+    at_row = lax.broadcasted_iota(jnp.int32, (CLS, ncls), 0)
+    at_col = lax.broadcasted_iota(jnp.int32, (CLS, ncls), 1)
+    bcol = jnp.sum(jnp.where(at_row == at_col, bout_ref[...], 0.0), axis=1, keepdims=True)
+    bcol = jnp.where(lax.broadcasted_iota(jnp.int32, (CLS, 1), 0) < ncls, bcol, -1e30)
     samples = GROUP * 2 * depth
+    low = lax.broadcasted_iota(jnp.int32, (depth // 8, 8, chans), 1) < 4
     run = 2 * depth
 
     def body(step, carry):
@@ -162,10 +175,10 @@
         a = jnp.tanh(u) + 1.0
         h = u * a
         hid = h.astype(BF16)
-        logits = dotg(wout_ref[...], hid, ((1,), (1,)))
+        logits = dotg(wout_t[...], hid, ((1,), (1,)))
         dparts = []
         for g in range(GROUP):
-            lt = logits[:, g * run:(g + 1) * run] + bout_ref[...]
+            lt = logits[:, g * run:(g + 1) * run] + bcol
             top = jnp.max(lt, axis=0, keepdims=True)
             e = jnp.exp(lt - top)
             inv = GRAD_SCALE / jnp.sum(e, axis=0, keepdims=True)
@@ -179,7 +192,7 @@
         for g in range(1, GROUP):
             tot += dparts[g].astype(F32)
         gbo_ref[...] += tot
-        dhh = dotg(dlt, wout_ref[...] * 0.5, ((0,), (0,)))
+        dhh = dotg(dlt, wout_t[...] * 0.5, ((0,), (0,)))
         q = (u + u + 1.0) - h
         dpre = (dhh * a * q).astype(BF16)
         lhs = jnp.concatenate([feats.T, jnp.ones((16, samples), BF16)], axis=0)
@@ -189,8 +202,10 @@
             slot, row, pair = spots[g]
             d = df[g * run:(g + 1) * run]
             zh_out[:, row] += (d[:depth] + d[depth:]).reshape(depth // 8, 8, chans)
+            d0, d1 = d[:depth].reshape(depth // 8, 8, chans), d[depth:].reshape(depth // 8, 8, chans)
+            wz_out[0, :, pair] += jnp.where(low, d0, pltpu.roll(d1, 4, 1))
+            wz_out[1, :, pair] += jnp.where(low, pltpu.roll(d0, 4, 1), d1)
             for p in range(2):
-                wz_out[:, 2 * pair + p] += d[p * depth:(p + 1) * depth].reshape(depth // 8, 8, chans)
                 hw_out[pl.ds(2 * slot + p, 1), :] = jnp.sum(d[p * depth:(p + 1) * depth], axis=0, keepdims=True)
         return carry
 
@@ -207,8 +222,6 @@
     rows, depth, chans = zh.shape
     pairs = wz.shape[0]
     hid, ncls = w_out.shape
-    wout = jnp.pad(w_out.T, ((0, CLS - ncls), (0, 0)))
-    bout = jnp.pad(b_out, (0, CLS - ncls), constant_values=-1e30).reshape(CLS, 1)
     smem = pl.BlockSpec(memory_space=pltpu.SMEM)
     vmem = pl.BlockSpec(memory_space=pltpu.VMEM)
     return pl.pallas_call(
@@ -216,7 +229,7 @@
         out_shape=(
             jax.ShapeDtypeStruct((2 * labels.shape[0], chans), F32),
             jax.ShapeDtypeStruct((depth // 8, rows, 8, chans), F32),
-            jax.ShapeDtypeStruct((depth // 8, 2 * pairs, 8, chans), F32),
+            jax.ShapeDtypeStruct((2, depth // 8, pairs, 8, chans), F32),
             jax.ShapeDtypeStruct((2 * (chans + 16) + 3 * CLS, chans), F32),
         ),
         in_specs=[smem] * 3 + [vmem] * 10,
@@ -224,12 +237,14 @@
         scratch_shapes=[
             pltpu.VMEM((hw.shape[0] + hwx.shape[0], chans), F32),
             pltpu.VMEM(labels.shape, jnp.int32),
+            pltpu.VMEM((CLS, hid), F32),
+            pltpu.VMEM((CLS, hid), BF16),
             pltpu.VMEM((chans + 16, hid), F32),
             pltpu.VMEM((CLS, hid), F32),
             pltpu.VMEM((CLS, 2 * depth), F32),
         ],
-        compiler_params=pltpu.CompilerParams(vmem_limit_bytes=48 * 1024 * 1024),
-    )(ids, idx, count, hw, hwx, zh, wz, labels, labx, w_in, b_in.reshape(1, hid), wout, bout)
+        compiler_params=pltpu.CompilerParams(vmem_limit_bytes=DECODE_VMEM),
+    )(ids, idx, count, hw, hwx, zh, wz, labels, labx, w_in, b_in.reshape(1, hid), w_out, b_out.reshape(1, ncls))
 
 
 def finish_kernel(
@@ -244,14 +259,17 @@
     hw_out[...] = jnp.zeros_like(hw_out)
 
     def put(source, start):
-        def go(s, carry):
-            for p in range(2):
-                hw_out[pl.ds(2 * ids_ref[0, start + s] + p, 1), :] = source[pl.ds(2 * s + p, 1), :]
+        def go(i, carry):
+            for k in range(8):
+                s = i * 8 + k
+                at = 2 * ids_ref[0, start + s]
+                for p in range(2):
+                    hw_out[pl.ds(at + p, 1), :] = source[pl.ds(2 * s + p, 1), :]
             return carry
         return go
 
-    lax.fori_loop(0, jnp.minimum(used, half), put(own_ref, 0), 0)
-    lax.fori_loop(0, jnp.maximum(used - half, 0), put(back_ref, half), 0)
+    lax.fori_loop(0, pl.cdiv(jnp.minimum(used, half), 8), put(own_ref, 0), 0)
+    lax.fori_loop(0, pl.cdiv(jnp.maximum(used - half, 0), 8), put(back_ref, half), 0)
     wz_out[...] = wz_ref[...]
     for i in range(8):
         zh_out[i] = zh_ref[:, i, :]
@@ -367,15 +385,14 @@
 
 def reduce_kernel(
     wz_ref, zh_ref, wt_ref, hw_ref, wz_out, zh_out, wt_out, hw_out,
-    wz_own, core_in, xsum, swap, zsum, wt_in, wt_mid,
-    own_sem, core_sem, swap_sem, wa_sem, wb_sem, wc_sem, *bufs,
+    wz_own, core_in, xsum, zsum, wt_in, wt_mid,
+    own_sem, core_sem, wa_sem, wb_sem, wc_sem, *bufs,
 ):
     xbufs, ybufs, zbufs, zybufs, hwbufs = (bufs[5 * i:5 * i + 5] for i in range(5))
     ha, wa = lax.axis_index("ha"), lax.axis_index("wa")
     yh, x, c = ha // 8, lax.rem(ha // 2, 4), lax.rem(ha, 2)
     yl, z = wa // 4, lax.rem(wa, 4)
-    half_w = wz_ref.shape[2] // 2
-    span = half_w // CHUNKS
+    span = wz_ref.shape[3] // CHUNKS
     n_ha, n_wa = wt_ref.shape[0], 8
 
     def on_x(to):
@@ -400,7 +417,7 @@
         pl.semaphore_signal(barrier, inc=1, device_id=(ha, lax.rem(wa + i, n_wa)), device_id_type=MESH)
         return carry
 
-    load = pltpu.make_async_copy(wz_ref.at[:, :, pl.ds(c * half_w, half_w)], wz_own, own_sem.at[0])
+    load = pltpu.make_async_copy(wz_ref.at[c], wz_own, own_sem.at[0])
     load.start()
     lax.fori_loop(1, n_ha, greet_ha, 0)
     lax.fori_loop(1, n_wa, greet_wa, 0)
@@ -413,7 +430,7 @@
             device_id=to, device_id_type=MESH)
 
     core = [
-        send(wz_ref.at[:, :, pl.ds((1 - c) * half_w + k * span, span)], core_in.at[:, :, pl.ds(k * span, span)],
+        send(wz_ref.at[1 - c, :, :, pl.ds(k * span, span)], core_in.at[:, :, pl.ds(k * span, span)],
              core_sem.at[k], sibling)
         for k in range(CHUNKS)
     ]
@@ -483,6 +500,12 @@
     start(wt_second, n_wa)
     for k in range(CHUNKS):
         rings[k].relay()
+    wait_slot(wt_mid, wb_sem, wa, n_wa, beside)
+    tot = wt_mid[0]
+    for i in range(1, n_wa):
+        tot += wt_mid[i]
+    wt_out[ha] = tot
+    start(wt_third, n_ha)
     zsum[0], zsum[1] = zring.finish()
     zys = [coded(zybufs, i, to) for i, to in enumerate((beside, corner, across))]
     zys[0].send(zsum[0, pl.ds(1 - yl, 1)])
@@ -495,34 +518,19 @@
         xsum[:, k, 0:span * 4], xsum[:, k, span * 4:] = lo, hi
         ys.append(coded(ybufs, k, across))
         ys[k].send(xsum[pl.ds(1 - yh, 1), k])
-    wait_slot(wt_mid, wb_sem, wa, n_wa, beside)
-    tot = wt_mid[0]
-    for i in range(1, n_wa):
-        tot += wt_mid[i]
-    wt_out[ha] = tot
-    start(wt_third, n_ha)
     total = zsum[0, pl.ds(yl, 1)]
     for m in zys:
         total += m.receive()
     zh_out[...] = total.reshape(zh_out.shape)
-    swaps = []
     for k in range(CHUNKS):
         rows = pl.ds(k * span, span)
-        r = (xsum[pl.ds(yh, 1), k] + ys[k].receive()).reshape(span, 8, chans)
-        mine = pl.ds(c * half_w + k * span, span)
-        wz_out[mine] = jnp.where(c == 0, r[:, :4], r[:, 4:])
-        swap[rows] = jnp.where(c == 0, r[:, 4:], r[:, :4])
-        swaps.append(send(swap.at[rows], wz_out.at[mine], swap_sem.at[k], sibling))
-        swaps[k].start()
+        wz_out[pl.ds(k * span, span)] = (xsum[pl.ds(yh, 1), k] + ys[k].receive()).reshape(span, 8, chans)
     hw_out[...] = back.receive().reshape(hw_out.shape)
-    for k in range(CHUNKS):
-        swaps[k].wait_recv()
     wait_slot(wt_out, wc_sem, ha, n_ha, sibling)
     for k in range(CHUNKS):
         core[k].wait_send()
         rings[k].done()
         ys[k].done()
-        swaps[k].wait_send()
     zring.done()
     for m in zys + [back]:
         m.done()
@@ -532,9 +540,8 @@
 
 
 def reduce_all(wz, zh, wt, hw):
-    width, chans = wz.shape[2], wz.shape[4]
+    half_w, chans = wz.shape[3], wz.shape[5]
     rows = zh.shape[2]
-    half_w = width // 2
     span = half_w // CHUNKS
     vmem = pl.BlockSpec(memory_space=pltpu.VMEM)
     buf = lambda *s: pltpu.VMEM(s, F32)
@@ -542,7 +549,7 @@
     return pl.pallas_call(
         reduce_kernel,
         out_shape=(
-            jax.ShapeDtypeStruct((width, 4, chans), F32),
+            jax.ShapeDtypeStruct((half_w, 8, chans), F32),
             jax.ShapeDtypeStruct((rows // 2, 8, chans), F32),
             jax.ShapeDtypeStruct(wt.shape, F32),
             jax.ShapeDtypeStruct((hw.shape[0] // 2, chans), F32),
@@ -553,11 +560,10 @@
             buf(2, 4, half_w, 8, chans),
             buf(2, 4, half_w, 8, chans),
             buf(2, CHUNKS, span * 8, chans),
-            buf(half_w, 4, chans),
             buf(2, 2, rows * 4, chans),
             buf(*wt.shape),
             buf(8, *wt.shape[1:]),
-            dma(1), dma(CHUNKS, 2), dma(CHUNKS, 2), dma(2, 16), dma(2, 8), dma(2, 16),
+            dma(1), dma(CHUNKS, 2), dma(2, 16), dma(2, 8), dma(2, 16),
             *coded_buffers(6 * CHUNKS, 2, span * 4, chans),
             *coded_buffers(CHUNKS, 1, span * 8, chans),
             *coded_buffers(6, 2, rows * 4, chans),
@@ -565,7 +571,7 @@
             *coded_buffers(1, hw.shape[0] // 256, 128, chans),
         ],
         compiler_params=pltpu.CompilerParams(
-            collective_id=0, has_side_effects=True, vmem_limit_bytes=48 * 1024 * 1024),
+            collective_id=0, has_side_effects=True, vmem_limit_bytes=REDUCE_VMEM),
     )(wz, zh, wt, hw)
 
 
@@ -573,18 +579,17 @@
     rows, cols, chans = hw_plane.shape
     depth = zh_plane.shape[0]
     ncls = w_out.shape[1]
-    zh_rows = jnp.transpose(zh_plane, (1, 0, 2))
     hw_rows = hw_plane.reshape(rows * cols, chans)
-    idx, hwx, zh2, labx = exchange(run_index, hw_rows, zh_rows, labels[0])
+    idx, hwx, zh2, labx = exchange(run_index, hw_rows, zh_plane, labels[0])
     hw, zh, wz, wt = decode_runs(
         run_index, idx, run_count, hw_rows, hwx, zh2, wz_plane.reshape(cols // 2, 2 * depth, chans),
         labels[0], labx, w_in, b_in, w_out, b_out,
     )
     wz_grad, zh_grad, wt, back = reduce_all(
-        wz.reshape(2, 4, cols, 8, chans), zh.reshape(2, 4, 2 * rows, 8, chans), wt.reshape(16, -1, chans), hw)
+        wz.reshape(2, 2, 4, cols // 2, 8, chans), zh.reshape(2, 4, 2 * rows, 8, chans), wt.reshape(16, -1, chans), hw)
     hw_grad, wz_grad, zh_grad, gwi, gbi, gwo, gbo = finish(
         run_index, run_count, hw, back, wz_grad, zh_grad, wt.reshape(-1, chans), rows * cols, w_out.shape[0], ncls)
-    return (hw_grad.reshape(rows, cols, chans), zh_grad, wz_grad, gwi, gbi[0], gwo, gbo[0])
+    return (hw_grad.reshape(rows, cols, chans), zh_grad, wz_grad.reshape(cols, 4, chans), gwi, gbi[0], gwo, gbo[0])
 
 
 def solution(mesh):

time: 100 us -> 93.3 us (0.933)
  Pallas kernels: 90.2 us -> 81.8 us
  local copies, waits for them, and re-layouts: 8.05 us -> 9.62 us
    pallas_call x1, Pallas kernels: 23.1 us -> 19.5 us  [exchange(): pl.pallas_call(exchange_kernel, out_shape=(jax.ShapeDtypeStruct(ids.shape...]
    unnamed x18 -> x24, local copies, waits for them, and re-layouts: 6.59 us -> 9.62 us
    pallas_call x1, Pallas kernels: 5.49 us -> 3.13 us  [finish(): pl.pallas_call(finish_kernel, out_shape=(jax.ShapeDtypeStruct((hw_rows, c...]
    pallas_call x1, Pallas kernels: 32.2 us -> 29.9 us  [decode_runs(): pl.pallas_call(decode_kernel, out_shape=(jax.ShapeDtypeStruct((2 * labels...]
where the time goes in v5:
time: 93.3 us; the launch traced here: 92.9 us
  Pallas kernels  81.8 us (88%)
  local copies, waits for them, and re-layouts  9.62 us (10%)
  between operations  1.45 us (2%)
    pallas_call x1, Pallas kernels, decode_runs(): pl.pallas_call(decode_kernel, out_shape=(jax.ShapeDtypeStruct((2 * labels...  29.9 us
    pallas_call x1, Pallas kernels, reduce_all(): pl.pallas_call(reduce_kernel, out_shape=(jax.ShapeDtypeStruct((half_w, 8,...  29.3 us
    pallas_call x1, Pallas kernels, exchange(): pl.pallas_call(exchange_kernel, out_shape=(jax.ShapeDtypeStruct(ids.shape...  19.5 us
    unnamed x24, local copies, waits for them, and re-layouts  9.62 us
    pallas_call x1, Pallas kernels, finish(): pl.pallas_call(finish_kernel, out_shape=(jax.ShapeDtypeStruct((hw_rows, c...  3.13 us

profile of v5, /device:TPU:0, one launch (start us, length us, event | category | flops | bytes accessed | tf_op | source)
XLA Modules:
  0.0 92.9 jit_solution(2614415191759758472)
XLA Ops:
  0.6 0.0 copy-start.3
  0.6 0.0 copy-start
  1.4 0.8 copy.17.wout_ref
  2.2 19.5 %shard_map.153 = (s32[1,512]{1,0:T(1,128)}, bf16[512,128]{1,0:T(8,128)(2,1)}, bf16[64,64,128]{2,1,0:T(8,128)(2,1)}, bf16[256,128]{1,0:T(8,128)(2,1)}) custom-call(s32[1,512]{1,0:T(1,128)} %ids_ref.5, s32[1,512]{1,0:T(1,128)} %ids_ref.5, bf16[4096,128]{1,0:T(8,128)(2,1)} %bitcast.13, bf16[64,32,128]{2,1,0:T(8,128)(2,1)} %zh_ref.1, s32[512,128]{1,0:T(8,128)} %bitcast.18), custom_call_target="tpu_custom_call" | custom-call | tf_op jit(solution)/shard_map/pallas_call | solution.py:101
  21.7 0.0 copy-done.3
  21.7 0.0 copy-done
  21.7 0.0 copy-start.1
  21.7 1.6 %copy-done.1 = bf16[128,64,128]{2,1,0:T(8,128)(2,1)S(1)} copy-done((bf16[128,64,128]{2,1,0:T(8,128)(2,1)S(1)}, bf16[128,64,128]{2,1,0:T(8,128)(2,1)}, u32[]{:S(2)}) %copy-start.1) | copy-done | bytes 2097176
  23.3 0.0 copy-start.2
  23.3 1.2 %copy-done.2 = bf16[64,64,128]{2,1,0:T(8,128)(2,1)S(1)} copy-done((bf16[64,64,128]{2,1,0:T(8,128)(2,1)S(1)}, bf16[64,64,128]{2,1,0:T(8,128)(2,1)}, u32[]{:S(2)}) %copy-start.2) | copy-done | bytes 1048600
  24.6 0.0 copy-start.4
  24.6 0.9 copy-done.4
  25.5 0.0 copy-start.5
  25.5 0.8 copy-done.5
  26.3 0.0 copy-start.6
  26.3 0.8 copy-done.6
  27.1 0.7 copy-done.7
  27.8 0.7 copy-done.8
  28.5 0.7 copy-done.9
  29.2 0.7 copy-done.10
  29.8 29.9 %shard_map.154 = (f32[1024,128]{1,0:T(8,128)S(1)}, f32[8,64,8,128]{3,2,1,0:T(8,128)S(1)}, f32[2,8,64,8,128]{4,3,2,1,0:T(8,128)S(1)}, f32[384,128]{1,0:T(8,128)S(1)}) custom-call(s32[1,512]{1,0:T(1,128)S(1)} %copy-done.7, s32[1,512]{1,0:T(1,128)S(1)} %copy-done.8, s32[1]{0:T(128)S(6)} %copy.19.count_ref, bf16[4096,128]{1,0:T(8,128)(2,1)S(1)} %bitcast.14, ...), custom_call_target="tpu_custom_call" | custom-call | tf_op jit(solution)/shard_map/pallas_call | solution.py:227
  59.8 29.3 %shard_map.155 = (f32[64,8,128]{2,1,0:T(8,128)S(1)}, f32[32,8,128]{2,1,0:T(8,128)S(1)}, f32[16,24,128]{2,1,0:T(8,128)S(1)}, f32[512,128]{1,0:T(8,128)S(1)}) custom-call(f32[2,2,4,64,8,128]{5,4,3,2,1,0:T(8,128)S(1)} %bitcast.15, f32[2,4,64,8,128]{4,3,2,1,0:T(8,128)S(1)} %bitcast.17, f32[16,24,128]{2,1,0:T(8,128)S(1)} %bitcast.20, ...), custom_call_target="tpu_custom_call" | custom-call | tf_op jit(solution)/shard_map/pallas_call | solution.py:549
  89.0 3.1 %shard_map.156 = (f32[4096,128]{1,0:T(8,128)}, f32[64,8,128]{2,1,0:T(8,128)}, f32[8,32,128]{2,1,0:T(8,128)}, f32[128,256]{1,0:T(8,128)}, f32[1,256]{1,0:T(1,128)...) custom-call(s32[1,512]{1,0:T(1,128)S(1)} %copy-done.7, s32[1]{0:T(128)S(6)} %copy.19.count_ref, ...), custom_call_target="tpu_custom_call" | custom-call | tf_op jit(solution)/shard_map/pallas_call | solution.py:291
  92.2 0.7 copy.18
  (4 shorter events, 0.0 us)
Async XLA Ops:
  0.6 21.1 %copy-start.3 = (s32[1,512,128]{2,1,0:T(8,128)S(1)}, s32[1,512,128]{2,1,0:T(8,128)}, u32[]{:S(2)}) copy-start(s32[1,512,128]{2,1,0:T(8,128)} %param.19) | copy-start | bytes 786436
  0.6 21.1 %copy-start = (bf16[32,128,128]{2,1,0:T(8,128)(2,1)S(1)}, bf16[32,128,128]{2,1,0:T(8,128)(2,1)}, u32[]{:S(2)}) copy-start(bf16[32,128,128]{2,1,0:T(8,128)(2,1)} %param.10) | copy-start | bytes 3145732
  21.7 1.6 %copy-start.1 = (bf16[128,64,128]{2,1,0:T(8,128)(2,1)S(1)}, bf16[128,64,128]{2,1,0:T(8,128)(2,1)}, u32[]{:S(2)}) copy-start(bf16[128,64,128]{2,1,0:T(8,128)(2,1)} %param.12) | copy-start | bytes 6291460
  23.3 1.2 %copy-start.2 = (bf16[64,64,128]{2,1,0:T(8,128)(2,1)S(1)}, bf16[64,64,128]{2,1,0:T(8,128)(2,1)}, u32[]{:S(2)}) copy-start(bf16[64,64,128]{2,1,0:T(8,128)(2,1)} %get-tuple-element.28.zh_ref) | copy-start | bytes 3145732
  24.6 0.9 copy-start.4
  25.5 0.8 copy-start.5
  26.3 0.8 copy-start.6
  27.1 0.7 copy-start.7
  27.8 0.7 copy-start.8
  28.5 0.7 copy-start.9
  29.2 0.7 copy-start.10

commit v6 on v5

--- a/solution.py
+++ b/solution.py
@@ -13,9 +13,10 @@
 GROUP = 32
 CLS = 32
 CHUNKS = 2
-EXCHANGE_VMEM = 56 * 1024 * 1024
-DECODE_VMEM = 40 * 1024 * 1024
-REDUCE_VMEM = 32 * 1024 * 1024
+EXCHANGE_VMEM = 58 * 1024 * 1024
+FINISH_VMEM = 58 * 1024 * 1024
+DECODE_VMEM = 58 * 1024 * 1024
+REDUCE_VMEM = 58 * 1024 * 1024
 MESH = pl.DeviceIdType.MESH
 
 
@@ -139,9 +140,9 @@
     gwi_ref[...] = jnp.zeros_like(gwi_ref)
     gwo_ref[...] = jnp.zeros_like(gwo_ref)
     gbo_ref[...] = jnp.zeros_like(gbo_ref)
-    ncls = wout_ref.shape[1]
+    ncls = wout_ref.shape[0]
     wpad[...] = jnp.zeros_like(wpad)
-    wpad[:ncls] = wout_ref[...].astype(F32).T
+    wpad[:ncls] = wout_ref[...].astype(F32)
     wout_t[...] = wpad[...].astype(BF16)
     at_row = lax.broadcasted_iota(jnp.int32, (CLS, ncls), 0)
     at_col = lax.broadcasted_iota(jnp.int32, (CLS, ncls), 1)
@@ -244,7 +245,7 @@
             pltpu.VMEM((CLS, 2 * depth), F32),
         ],
         compiler_params=pltpu.CompilerParams(vmem_limit_bytes=DECODE_VMEM),
-    )(ids, idx, count, hw, hwx, zh, wz, labels, labx, w_in, b_in.reshape(1, hid), w_out, b_out.reshape(1, ncls))
+    )(ids, idx, count, hw, hwx, zh, wz, labels, labx, w_in, b_in.reshape(1, hid), w_out.T, b_out.reshape(1, ncls))
 
 
 def finish_kernel(
@@ -255,7 +256,7 @@
     half = cap // 2
     used = count_ref[0]
     chans = hw_out.shape[1]
-    ncls = gwo_out.shape[1]
+    ncls = gwo_out.shape[0]
     hw_out[...] = jnp.zeros_like(hw_out)
 
     def put(source, start):
@@ -279,8 +280,8 @@
     gbi_out[:, :128] = wt_ref[chans:chans + 1]
     gbi_out[:, 128:] = wt_ref[top + chans:top + chans + 1]
     at = 2 * top
-    gwo_out[:128] = wt_ref[at:at + CLS].T[:, :ncls]
-    gwo_out[128:] = wt_ref[at + CLS:at + 2 * CLS].T[:, :ncls]
+    gwo_out[:, :128] = wt_ref[at:at + ncls]
+    gwo_out[:, 128:] = wt_ref[at + CLS:at + CLS + ncls]
     gbo_out[...] = jnp.sum(wt_ref[at + 2 * CLS:at + 3 * CLS].T, axis=0, keepdims=True)[:, :ncls]
 
 
@@ -296,12 +297,12 @@
             jax.ShapeDtypeStruct((8, zh.shape[0], chans), F32),
             jax.ShapeDtypeStruct((chans, hid), F32),
             jax.ShapeDtypeStruct((1, hid), F32),
-            jax.ShapeDtypeStruct((hid, ncls), F32),
+            jax.ShapeDtypeStruct((ncls, hid), F32),
             jax.ShapeDtypeStruct((1, ncls), F32),
         ),
         in_specs=[smem] * 2 + [vmem] * 5,
         out_specs=[vmem] * 7,
-        compiler_params=pltpu.CompilerParams(vmem_limit_bytes=32 * 1024 * 1024),
+        compiler_params=pltpu.CompilerParams(vmem_limit_bytes=FINISH_VMEM),
     )(ids, count, own, back, wz, zh, wt)
 
 
@@ -384,8 +385,8 @@
 
 
 def reduce_kernel(
-    wz_ref, zh_ref, wt_ref, hw_ref, wz_out, zh_out, wt_out, hw_out,
-    wz_own, core_in, xsum, zsum, wt_in, wt_mid,
+    wz_ref, zh_hbm, wt_ref, hw_hbm, wz_out, zh_out, wt_out, hw_out,
+    wz_own, zh_ref, hw_ref, core_in, xsum, zsum, wt_in, wt_mid,
     own_sem, core_sem, wa_sem, wb_sem, wc_sem, *bufs,
 ):
     xbufs, ybufs, zbufs, zybufs, hwbufs = (bufs[5 * i:5 * i + 5] for i in range(5))
@@ -417,8 +418,13 @@
         pl.semaphore_signal(barrier, inc=1, device_id=(ha, lax.rem(wa + i, n_wa)), device_id_type=MESH)
         return carry
 
-    load = pltpu.make_async_copy(wz_ref.at[c], wz_own, own_sem.at[0])
-    load.start()
+    loads = [
+        pltpu.make_async_copy(zh_hbm, zh_ref, own_sem.at[0]),
+        pltpu.make_async_copy(hw_hbm.at[pl.ds(hw_out.shape[0], hw_out.shape[0])], hw_ref, own_sem.at[1]),
+        pltpu.make_async_copy(wz_ref.at[c], wz_own, own_sem.at[2]),
+    ]
+    for cp in loads:
+        cp.start()
     lax.fori_loop(1, n_ha, greet_ha, 0)
     lax.fori_loop(1, n_wa, greet_wa, 0)
     pl.semaphore_signal(barrier, inc=1, device_id=corner, device_id_type=MESH)
@@ -437,6 +443,7 @@
     for k in range(CHUNKS):
         core[k].start()
     zring = Ring(zh_ref, zbufs, 0, on_z, z, zh_ref.shape[2], 0)
+    loads[0].wait()
     zring.begin()
 
     def wt_first(i):
@@ -481,8 +488,9 @@
     start(wt_first, n_ha)
     chans = hw_ref.shape[1]
     back = coded(hwbufs, 0, across)
-    back.send(hw_ref[hw_out.shape[0]:].reshape(-1, 128, chans))
-    load.wait()
+    loads[1].wait()
+    back.send(hw_ref[...].reshape(-1, 128, chans))
+    loads[2].wait()
     rings = []
     for k in range(CHUNKS):
         rows = pl.ds(k * span, span)
@@ -544,6 +552,7 @@
     rows = zh.shape[2]
     span = half_w // CHUNKS
     vmem = pl.BlockSpec(memory_space=pltpu.VMEM)
+    hbm = pl.BlockSpec(memory_space=pl.ANY)
     buf = lambda *s: pltpu.VMEM(s, F32)
     dma = lambda *s: pltpu.SemaphoreType.DMA(s)
     return pl.pallas_call(
@@ -554,16 +563,18 @@
             jax.ShapeDtypeStruct(wt.shape, F32),
             jax.ShapeDtypeStruct((hw.shape[0] // 2, chans), F32),
         ),
-        in_specs=[pl.BlockSpec(memory_space=pl.ANY)] + [vmem] * 3,
+        in_specs=[hbm, hbm, vmem, hbm],
         out_specs=[vmem] * 4,
         scratch_shapes=[
             buf(2, 4, half_w, 8, chans),
+            buf(*zh.shape),
+            buf(hw.shape[0] // 2, chans),
             buf(2, 4, half_w, 8, chans),
             buf(2, CHUNKS, span * 8, chans),
             buf(2, 2, rows * 4, chans),
             buf(*wt.shape),
             buf(8, *wt.shape[1:]),
-            dma(1), dma(CHUNKS, 2), dma(2, 16), dma(2, 8), dma(2, 16),
+            dma(3), dma(CHUNKS, 2), dma(2, 16), dma(2, 8), dma(2, 16),
             *coded_buffers(6 * CHUNKS, 2, span * 4, chans),
             *coded_buffers(CHUNKS, 1, span * 8, chans),
             *coded_buffers(6, 2, rows * 4, chans),
@@ -589,7 +600,7 @@
         wz.reshape(2, 2, 4, cols // 2, 8, chans), zh.reshape(2, 4, 2 * rows, 8, chans), wt.reshape(16, -1, chans), hw)
     hw_grad, wz_grad, zh_grad, gwi, gbi, gwo, gbo = finish(
         run_index, run_count, hw, back, wz_grad, zh_grad, wt.reshape(-1, chans), rows * cols, w_out.shape[0], ncls)
-    return (hw_grad.reshape(rows, cols, chans), zh_grad, wz_grad.reshape(cols, 4, chans), gwi, gbi[0], gwo, gbo[0])
+    return (hw_grad.reshape(rows, cols, chans), zh_grad, wz_grad.reshape(cols, 4, chans), gwi, gbi[0], gwo.T, gbo[0])
 
 
 def solution(mesh):

time: 93.3 us -> 90.1 us (0.966)
  local copies, waits for them, and re-layouts: 9.62 us -> 0 us
  Pallas kernels: 81.8 us -> 88.6 us
    unnamed x24 -> x0, local copies, waits for them, and re-layouts: 9.62 us -> none
    pallas_call x1, Pallas kernels: 29.9 us -> 34.5 us  [decode_runs(): pl.pallas_call(decode_kernel, out_shape=(jax.ShapeDtypeStruct((2 * labels...]
    pallas_call x1, Pallas kernels: 29.3 us -> 30.8 us  [reduce_all(): pl.pallas_call(reduce_kernel, out_shape=(jax.ShapeDtypeStruct((half_w, 8,...]
where the time goes in v6:
time: 90.1 us; the launch traced here: 89.9 us
  Pallas kernels  88.6 us (98%)
  between operations  1.3 us (1%)
    pallas_call x1, Pallas kernels, decode_runs(): pl.pallas_call(decode_kernel, out_shape=(jax.ShapeDtypeStruct((2 * labels...  34.5 us
    pallas_call x1, Pallas kernels, reduce_all(): pl.pallas_call(reduce_kernel, out_shape=(jax.ShapeDtypeStruct((half_w, 8,...  30.8 us
    pallas_call x1, Pallas kernels, exchange(): pl.pallas_call(exchange_kernel, out_shape=(jax.ShapeDtypeStruct(ids.shape...  19.5 us
    pallas_call x1, Pallas kernels, finish(): pl.pallas_call(finish_kernel, out_shape=(jax.ShapeDtypeStruct((hw_rows, c...  3.85 us

profile of v6, /device:TPU:0, one launch (start us, length us, event | category | flops | bytes accessed | tf_op | source)
XLA Modules:
  0.0 89.9 jit_solution(17722157143833456583)
XLA Ops:
  1.3 19.5 %shard_map.153 = (s32[1,512]{1,0:T(1,128)}, bf16[512,128]{1,0:T(8,128)(2,1)}, bf16[64,64,128]{2,1,0:T(8,128)(2,1)}, bf16[256,128]{1,0:T(8,128)(2,1)}) custom-call(s32[1,512]{1,0:T(1,128)} %ids_ref.5, s32[1,512]{1,0:T(1,128)} %ids_ref.5, bf16[4096,128]{1,0:T(8,128)(2,1)} %bitcast.16, bf16[64,32,128]{2,1,0:T(8,128)(2,1)} %zh_ref.1, s32[512,128]{1,0:T(8,128)} %bitcast.20), custom_call_target="tpu_custom_call" | custom-call | tf_op jit(solution)/shard_map/pallas_call | solution.py:102
  20.8 34.5 %shard_map.154 = (f32[1024,128]{1,0:T(8,128)}, f32[8,64,8,128]{3,2,1,0:T(8,128)}, f32[2,8,64,8,128]{4,3,2,1,0:T(8,128)}, f32[384,128]{1,0:T(8,128)}) custom-call(s32[1,512]{1,0:T(1,128)} %ids_ref.5, s32[1,512]{1,0:T(1,128)} %get-tuple-element.26.idx_ref, s32[1]{0:T(128)S(6)} %copy.17.count_ref, bf16[4096,128]{1,0:T(8,128)(2,1)} %bitcast.17, ...), custom_call_target="tpu_custom_call" | custom-call | tf_op jit(solution)/shard_map/pallas_call | solution.py:228
  55.2 30.8 %shard_map.155 = (f32[64,8,128]{2,1,0:T(8,128)}, f32[32,8,128]{2,1,0:T(8,128)}, f32[16,24,128]{2,1,0:T(8,128)}, f32[512,128]{1,0:T(8,128)}) custom-call(f32[2,2,4,64,8,128]{5,4,3,2,1,0:T(8,128)} %bitcast.15, f32[2,4,64,8,128]{4,3,2,1,0:T(8,128)} %bitcast.19, f32[16,24,128]{2,1,0:T(8,128)} %bitcast.22, f32[1024,128]{1,0:T(8,128)} %get-tuple-element.30.hw_hbm.own_ref), custom_call_target="tpu_custom_call" | custom-call | tf_op jit(solution)/shard_map/pallas_call | solution.py:558
  86.1 3.8 %shard_map.156 = (f32[4096,128]{1,0:T(8,128)}, f32[64,8,128]{2,1,0:T(8,128)}, f32[8,32,128]{2,1,0:T(8,128)}, f32[128,256]{1,0:T(8,128)}, f32[1,256]{1,0:T(1,128)}, /*index=5*/f32[18,256]{1,0:T(8,128)}, f32[1,18]{1,0:T(1,128)}) custom-call(s32[1,512]{1,0:T(1,128)} %ids_ref.5, s32[1]{0:T(128)S(6)} %copy.17.count_ref, ...), custom_call_target="tpu_custom_call" | custom-call | tf_op jit(solution)/shard_map/pallas_call | solution.py:292

commit v7 on v6

--- a/solution.py
+++ b/solution.py
@@ -10,7 +10,7 @@
 F32 = jnp.float32
 BF16 = jnp.bfloat16
 GRAD_SCALE = 0.25
-GROUP = 32
+GROUP = 64
 CLS = 32
 CHUNKS = 2
 EXCHANGE_VMEM = 58 * 1024 * 1024
@@ -179,14 +179,14 @@
         logits = dotg(wout_t[...], hid, ((1,), (1,)))
         dparts = []
         for g in range(GROUP):
-            lt = logits[:, g * run:(g + 1) * run] + bcol
+            lt = logits[:24, g * run:(g + 1) * run] + bcol[:24]
             top = jnp.max(lt, axis=0, keepdims=True)
             e = jnp.exp(lt - top)
             inv = GRAD_SCALE / jnp.sum(e, axis=0, keepdims=True)
             lab = labs[pl.ds(spots[g][0], 1), :]
             cls = lax.broadcasted_iota(jnp.int32, lt.shape, 0)
             hot = jnp.where(cls == lab, GRAD_SCALE, 0.0)
-            dparts.append((e * inv - hot).astype(BF16))
+            dparts.append(jnp.concatenate([e * inv - hot, jnp.zeros((CLS - 24, run), F32)], axis=0).astype(BF16))
         dlt = jnp.concatenate(dparts, axis=1)
         gwo_ref[...] += jnp.dot(dlt, hid, preferred_element_type=F32)
         tot = dparts[0].astype(F32)
@@ -197,7 +197,6 @@
         q = (u + u + 1.0) - h
         dpre = (dhh * a * q).astype(BF16)
         lhs = jnp.concatenate([feats.T, jnp.ones((16, samples), BF16)], axis=0)
-        gwi_ref[...] += jnp.dot(lhs, dpre, preferred_element_type=F32)
         df = dotg(dpre, win_ref[...], ((1,), (1,)))
         for g in range(GROUP):
             slot, row, pair = spots[g]
@@ -208,6 +207,7 @@
             wz_out[1, :, pair] += jnp.where(low, pltpu.roll(d0, 4, 1), d1)
             for p in range(2):
                 hw_out[pl.ds(2 * slot + p, 1), :] = jnp.sum(d[p * depth:(p + 1) * depth], axis=0, keepdims=True)
+        gwi_ref[...] += jnp.dot(lhs, dpre, preferred_element_type=F32)
         return carry
 
     lax.fori_loop(0, half // GROUP, body, 0)
@@ -306,50 +306,48 @@
     )(ids, count, own, back, wz, zh, wt)
 
 
+TAIL = 16
+
+
 def pack(v):
     most = jnp.maximum(jnp.max(jnp.abs(v), axis=1, keepdims=True), 1e-30)
-    return jnp.round(v * (32766.0 / most)).astype(jnp.int32).astype(jnp.int16), most * (1.0 / 32766.0)
-
-
-def unpack(q, scale):
-    return q.astype(jnp.int32).astype(F32) * scale
+    power = jnp.ceil(jnp.log2(most))
+    q = jnp.round(v * (jnp.exp2(-power) * 32600.0)).astype(jnp.int32).astype(jnp.int16)
+    tail = jnp.broadcast_to(power, (v.shape[0], TAIL, v.shape[2])).astype(jnp.int32).astype(jnp.int16)
+    return q, tail
+
+
+def unpack(q, tail):
+    power = tail.astype(jnp.int32).astype(F32)[:, :1]
+    return q.astype(jnp.int32).astype(F32) * (jnp.exp2(power) * (1.0 / 32600.0))
 
 
 class Coded:
-    def __init__(self, out, out_scale, into, into_scale, sems, to):
-        self.out, self.out_scale, self.into, self.into_scale = out, out_scale, into, into_scale
-        self.copies = [
-            pltpu.make_async_remote_copy(
-                src_ref=a, dst_ref=b, send_sem=sems.at[0, i], recv_sem=sems.at[1, i], device_id=to, device_id_type=MESH)
-            for i, (a, b) in enumerate(((out, into), (out_scale, into_scale)))
-        ]
+    def __init__(self, out, into, sems, to):
+        self.out, self.into, self.rows = out, into, out.shape[1] - TAIL
+        self.copy = pltpu.make_async_remote_copy(
+            src_ref=out, dst_ref=into, send_sem=sems.at[0], recv_sem=sems.at[1], device_id=to, device_id_type=MESH)
 
     def send(self, v):
-        self.out[...], self.out_scale[...] = pack(v)
-        for cp in self.copies:
-            cp.start()
+        self.out[:, :self.rows], self.out[:, self.rows:] = pack(v)
+        self.copy.start()
 
     def receive(self):
-        for cp in self.copies:
-            cp.wait_recv()
-        return unpack(self.into[...], self.into_scale[...])
+        self.copy.wait_recv()
+        return unpack(self.into[:, :self.rows], self.into[:, self.rows:])
 
     def done(self):
-        for cp in self.copies:
-            cp.wait_send()
+        self.copy.wait_send()
 
 
 def coded_buffers(n, groups, rows, chans):
-    return [
-        pltpu.VMEM((n, groups, rows, chans), jnp.int16), pltpu.VMEM((n, groups, 1, chans), F32),
-        pltpu.VMEM((n, groups, rows, chans), jnp.int16), pltpu.VMEM((n, groups, 1, chans), F32),
-        pltpu.SemaphoreType.DMA((n, 2, 2)),
-    ]
+    shape = (n, groups, rows + TAIL, chans)
+    return [pltpu.VMEM(shape, jnp.int16), pltpu.VMEM(shape, jnp.int16), pltpu.SemaphoreType.DMA((n, 2))]
 
 
 def coded(bufs, i, to):
-    out, out_scale, into, into_scale, sems = bufs
-    return Coded(out.at[i], out_scale.at[i], into.at[i], into_scale.at[i], sems.at[i], to)
+    out, into, sems = bufs
+    return Coded(out.at[i], into.at[i], sems.at[i], to)
 
 
 class Ring:
@@ -389,7 +387,7 @@
     wz_own, zh_ref, hw_ref, core_in, xsum, zsum, wt_in, wt_mid,
     own_sem, core_sem, wa_sem, wb_sem, wc_sem, *bufs,
 ):
-    xbufs, ybufs, zbufs, zybufs, hwbufs = (bufs[5 * i:5 * i + 5] for i in range(5))
+    xbufs, ybufs, zbufs, zybufs, hwbufs = (bufs[3 * i:3 * i + 3] for i in range(5))
     ha, wa = lax.axis_index("ha"), lax.axis_index("wa")
     yh, x, c = ha // 8, lax.rem(ha // 2, 4), lax.rem(ha, 2)
     yl, z = wa // 4, lax.rem(wa, 4)
@@ -449,19 +447,19 @@
     def wt_first(i):
         to = lax.rem(ha + i, n_ha)
         return pltpu.make_async_remote_copy(
-            src_ref=wt_ref.at[to], dst_ref=wt_in.at[ha], send_sem=wa_sem.at[0, to], recv_sem=wa_sem.at[1, ha],
+            src_ref=wt_ref.at[to], dst_ref=wt_in.at[ha], send_sem=wa_sem.at[0], recv_sem=wa_sem.at[1],
             device_id=(to, wa), device_id_type=MESH)
 
     def wt_second(i):
         to = lax.rem(wa + i, n_wa)
         return pltpu.make_async_remote_copy(
-            src_ref=wt_mid.at[wa], dst_ref=wt_mid.at[wa], send_sem=wb_sem.at[0, to], recv_sem=wb_sem.at[1, wa],
+            src_ref=wt_mid.at[wa], dst_ref=wt_mid.at[wa], send_sem=wb_sem.at[0], recv_sem=wb_sem.at[1],
             device_id=(ha, to), device_id_type=MESH)
 
     def wt_third(i):
         to = lax.rem(ha + i, n_ha)
         return pltpu.make_async_remote_copy(
-            src_ref=wt_out.at[ha], dst_ref=wt_out.at[ha], send_sem=wc_sem.at[0, to], recv_sem=wc_sem.at[1, ha],
+            src_ref=wt_out.at[ha], dst_ref=wt_out.at[ha], send_sem=wc_sem.at[0], recv_sem=wc_sem.at[1],
             device_id=(to, wa), device_id_type=MESH)
 
     def start(make, n):
@@ -470,21 +468,13 @@
             return carry
         lax.fori_loop(1, n, go, 0)
 
-    def wait_send(make, n):
-        def go(i, carry):
-            make(i).wait_send()
-            return carry
-        lax.fori_loop(1, n, go, 0)
-
-    def wait_slot(buf, sems, me, n, own):
-        def go(i, carry):
-            frm = lax.rem(me + i, n)
-            pltpu.make_async_remote_copy(
-                src_ref=buf.at[frm], dst_ref=buf.at[frm], send_sem=sems.at[0, frm], recv_sem=sems.at[1, frm],
-                device_id=own, device_id_type=MESH).wait_recv()
-            return carry
-        lax.fori_loop(1, n, go, 0)
-
+    def all_of(buf, sems, n, to):
+        many = buf.at[pl.ds(0, n - 1)]
+        return pltpu.make_async_remote_copy(
+            src_ref=many, dst_ref=many, send_sem=sems.at[0], recv_sem=sems.at[1], device_id=to, device_id_type=MESH)
+
+    first_all, second_all, third_all = (
+        all_of(wt_in, wa_sem, n_ha, sibling), all_of(wt_mid, wb_sem, n_wa, beside), all_of(wt_out, wc_sem, n_ha, sibling))
     start(wt_first, n_ha)
     chans = hw_ref.shape[1]
     back = coded(hwbufs, 0, across)
@@ -499,7 +489,7 @@
         rings.append(Ring(core_in, xbufs, 6 * k, on_x, x, span, k * span))
         rings[k].begin()
     zring.relay()
-    wait_slot(wt_in, wa_sem, ha, n_ha, sibling)
+    first_all.wait_recv()
     wt_in[ha] = wt_ref[ha]
     tot = wt_in[0]
     for i in range(1, n_ha):
@@ -508,7 +498,7 @@
     start(wt_second, n_wa)
     for k in range(CHUNKS):
         rings[k].relay()
-    wait_slot(wt_mid, wb_sem, wa, n_wa, beside)
+    second_all.wait_recv()
     tot = wt_mid[0]
     for i in range(1, n_wa):
         tot += wt_mid[i]
@@ -534,7 +524,7 @@
         rows = pl.ds(k * span, span)
         wz_out[pl.ds(k * span, span)] = (xsum[pl.ds(yh, 1), k] + ys[k].receive()).reshape(span, 8, chans)
     hw_out[...] = back.receive().reshape(hw_out.shape)
-    wait_slot(wt_out, wc_sem, ha, n_ha, sibling)
+    third_all.wait_recv()
     for k in range(CHUNKS):
         core[k].wait_send()
         rings[k].done()
@@ -542,9 +532,8 @@
     zring.done()
     for m in zys + [back]:
         m.done()
-    wait_send(wt_first, n_ha)
-    wait_send(wt_second, n_wa)
-    wait_send(wt_third, n_ha)
+    for cp in (first_all, second_all, third_all):
+        cp.wait_send()
 
 
 def reduce_all(wz, zh, wt, hw):
@@ -574,7 +563,7 @@
             buf(2, 2, rows * 4, chans),
             buf(*wt.shape),
             buf(8, *wt.shape[1:]),
-            dma(3), dma(CHUNKS, 2), dma(2, 16), dma(2, 8), dma(2, 16),
+            dma(3), dma(CHUNKS, 2), dma(2), dma(2), dma(2),
             *coded_buffers(6 * CHUNKS, 2, span * 4, chans),
             *coded_buffers(CHUNKS, 1, span * 8, chans),
             *coded_buffers(6, 2, rows * 4, chans),

time: 90.1 us -> 87.9 us (0.976)
  Pallas kernels: 88.6 us -> 86.3 us
    pallas_call x1, Pallas kernels: 34.5 us -> 33 us  [decode_runs(): pl.pallas_call(decode_kernel, out_shape=(jax.ShapeDtypeStruct((2 * labels...]
where the time goes in v7:
time: 87.9 us; the launch traced here: 87.6 us
  Pallas kernels  86.3 us (98%)
  between operations  1.3 us (1%)
    pallas_call x1, Pallas kernels, decode_runs(): pl.pallas_call(decode_kernel, out_shape=(jax.ShapeDtypeStruct((2 * labels...  33 us
    pallas_call x1, Pallas kernels, reduce_all(): pl.pallas_call(reduce_kernel, out_shape=(jax.ShapeDtypeStruct((half_w, 8,...  30 us
    pallas_call x1, Pallas kernels, exchange(): pl.pallas_call(exchange_kernel, out_shape=(jax.ShapeDtypeStruct(ids.shape...  19.5 us
    pallas_call x1, Pallas kernels, finish(): pl.pallas_call(finish_kernel, out_shape=(jax.ShapeDtypeStruct((hw_rows, c...  3.85 us

profile of v7, /device:TPU:0, one launch (start us, length us, event | category | flops | bytes accessed | tf_op | source)
XLA Modules:
  0.0 87.6 jit_solution(479009522310720572)
XLA Ops:
  1.3 19.5 %shard_map.153 = (s32[1,512]{1,0:T(1,128)}, bf16[512,128]{1,0:T(8,128)(2,1)}, bf16[64,64,128]{2,1,0:T(8,128)(2,1)}, bf16[256,128]{1,0:T(8,128)(2,1)}) custom-call(s32[1,512]{1,0:T(1,128)} %ids_ref.5, s32[1,512]{1,0:T(1,128)} %ids_ref.5, bf16[4096,128]{1,0:T(8,128)(2,1)} %bitcast.16, bf16[64,32,128]{2,1,0:T(8,128)(2,1)} %zh_ref.1, s32[512,128]{1,0:T(8,128)} %bitcast.20), custom_call_target="tpu_custom_call" | custom-call | tf_op jit(solution)/shard_map/pallas_call | solution.py:102
  20.8 33.0 %shard_map.154 = (f32[1024,128]{1,0:T(8,128)}, f32[8,64,8,128]{3,2,1,0:T(8,128)}, f32[2,8,64,8,128]{4,3,2,1,0:T(8,128)}, f32[384,128]{1,0:T(8,128)}) custom-call(s32[1,512]{1,0:T(1,128)} %ids_ref.5, s32[1,512]{1,0:T(1,128)} %get-tuple-element.26.idx_ref, s32[1]{0:T(128)S(6)} %copy.17.count_ref, bf16[4096,128]{1,0:T(8,128)(2,1)} %bitcast.17, ...), custom_call_target="tpu_custom_call" | custom-call | tf_op jit(solution)/shard_map/pallas_call | solution.py:228
  53.8 30.0 %shard_map.155 = (f32[64,8,128]{2,1,0:T(8,128)}, f32[32,8,128]{2,1,0:T(8,128)}, f32[16,24,128]{2,1,0:T(8,128)}, f32[512,128]{1,0:T(8,128)}) custom-call(f32[2,2,4,64,8,128]{5,4,3,2,1,0:T(8,128)} %bitcast.15, f32[2,4,64,8,128]{4,3,2,1,0:T(8,128)} %bitcast.19, f32[16,24,128]{2,1,0:T(8,128)} %bitcast.22, f32[1024,128]{1,0:T(8,128)} %get-tuple-element.30.hw_hbm.own_ref), custom_call_target="tpu_custom_call" | custom-call | tf_op jit(solution)/shard_map/pallas_call | solution.py:547
  83.8 3.8 %shard_map.156 = (f32[4096,128]{1,0:T(8,128)}, f32[64,8,128]{2,1,0:T(8,128)}, f32[8,32,128]{2,1,0:T(8,128)}, f32[128,256]{1,0:T(8,128)}, f32[1,256]{1,0:T(1,128)}, /*index=5*/f32[18,256]{1,0:T(8,128)}, f32[1,18]{1,0:T(1,128)}) custom-call(s32[1,512]{1,0:T(1,128)} %ids_ref.5, s32[1]{0:T(128)S(6)} %copy.17.count_ref, ...), custom_call_target="tpu_custom_call" | custom-call | tf_op jit(solution)/shard_map/pallas_call | solution.py:292

commit v8 on v7

--- a/solution.py
+++ b/solution.py
@@ -384,8 +384,8 @@
 
 def reduce_kernel(
     wz_ref, zh_hbm, wt_ref, hw_hbm, wz_out, zh_out, wt_out, hw_out,
-    wz_own, zh_ref, hw_ref, core_in, xsum, zsum, wt_in, wt_mid,
-    own_sem, core_sem, wa_sem, wb_sem, wc_sem, *bufs,
+    wz_own, zh_ref, hw_ref, core_in, xsum, zsum, wt_core, wt_in, wt_mid,
+    own_sem, core_sem, wa_sem, wb_sem, wc_sem, wd_sem, we_sem, *bufs,
 ):
     xbufs, ybufs, zbufs, zybufs, hwbufs = (bufs[3 * i:3 * i + 3] for i in range(5))
     ha, wa = lax.axis_index("ha"), lax.axis_index("wa")
@@ -438,6 +438,11 @@
              core_sem.at[k], sibling)
         for k in range(CHUNKS)
     ]
+    peers = n_ha // 2
+    group = ha // 2
+    wt_own = pl.ds(c * peers, peers)
+    wt_swap = send(wt_ref.at[pl.ds((1 - c) * peers, peers)], wt_core, wd_sem, sibling)
+    wt_swap.start()
     for k in range(CHUNKS):
         core[k].start()
     zring = Ring(zh_ref, zbufs, 0, on_z, z, zh_ref.shape[2], 0)
@@ -445,10 +450,10 @@
     zring.begin()
 
     def wt_first(i):
-        to = lax.rem(ha + i, n_ha)
+        to = lax.rem(group + i, peers)
         return pltpu.make_async_remote_copy(
-            src_ref=wt_ref.at[to], dst_ref=wt_in.at[ha], send_sem=wa_sem.at[0], recv_sem=wa_sem.at[1],
-            device_id=(to, wa), device_id_type=MESH)
+            src_ref=wt_core.at[to], dst_ref=wt_in.at[group], send_sem=wa_sem.at[0], recv_sem=wa_sem.at[1],
+            device_id=(to * 2 + c, wa), device_id_type=MESH)
 
     def wt_second(i):
         to = lax.rem(wa + i, n_wa)
@@ -457,10 +462,11 @@
             device_id=(ha, to), device_id_type=MESH)
 
     def wt_third(i):
-        to = lax.rem(ha + i, n_ha)
+        to = lax.rem(group + i, peers)
+        piece = wt_out.at[c * peers + group]
         return pltpu.make_async_remote_copy(
-            src_ref=wt_out.at[ha], dst_ref=wt_out.at[ha], send_sem=wc_sem.at[0], recv_sem=wc_sem.at[1],
-            device_id=(to, wa), device_id_type=MESH)
+            src_ref=piece, dst_ref=piece, send_sem=wc_sem.at[0], recv_sem=wc_sem.at[1],
+            device_id=(to * 2 + c, wa), device_id_type=MESH)
 
     def start(make, n):
         def go(i, carry):
@@ -474,8 +480,10 @@
             src_ref=many, dst_ref=many, send_sem=sems.at[0], recv_sem=sems.at[1], device_id=to, device_id_type=MESH)
 
     first_all, second_all, third_all = (
-        all_of(wt_in, wa_sem, n_ha, sibling), all_of(wt_mid, wb_sem, n_wa, beside), all_of(wt_out, wc_sem, n_ha, sibling))
-    start(wt_first, n_ha)
+        all_of(wt_in, wa_sem, peers, sibling), all_of(wt_mid, wb_sem, n_wa, beside), all_of(wt_out, wc_sem, peers, sibling))
+    wt_swap.wait_recv()
+    wt_core[...] += wt_ref[wt_own]
+    start(wt_first, peers)
     chans = hw_ref.shape[1]
     back = coded(hwbufs, 0, across)
     loads[1].wait()
@@ -490,9 +498,9 @@
         rings[k].begin()
     zring.relay()
     first_all.wait_recv()
-    wt_in[ha] = wt_ref[ha]
+    wt_in[group] = wt_core[group]
     tot = wt_in[0]
-    for i in range(1, n_ha):
+    for i in range(1, peers):
         tot += wt_in[i]
     wt_mid[wa] = tot
     start(wt_second, n_wa)
@@ -502,8 +510,8 @@
     tot = wt_mid[0]
     for i in range(1, n_wa):
         tot += wt_mid[i]
-    wt_out[ha] = tot
-    start(wt_third, n_ha)
+    wt_out[c * peers + group] = tot
+    start(wt_third, peers)
     zsum[0], zsum[1] = zring.finish()
     zys = [coded(zybufs, i, to) for i, to in enumerate((beside, corner, across))]
     zys[0].send(zsum[0, pl.ds(1 - yl, 1)])
@@ -516,6 +524,9 @@
         xsum[:, k, 0:span * 4], xsum[:, k, span * 4:] = lo, hi
         ys.append(coded(ybufs, k, across))
         ys[k].send(xsum[pl.ds(1 - yh, 1), k])
+    third_all.wait_recv()
+    wt_last = send(wt_out.at[wt_own], wt_out.at[wt_own], we_sem, sibling)
+    wt_last.start()
     total = zsum[0, pl.ds(yl, 1)]
     for m in zys:
         total += m.receive()
@@ -524,7 +535,6 @@
         rows = pl.ds(k * span, span)
         wz_out[pl.ds(k * span, span)] = (xsum[pl.ds(yh, 1), k] + ys[k].receive()).reshape(span, 8, chans)
     hw_out[...] = back.receive().reshape(hw_out.shape)
-    third_all.wait_recv()
     for k in range(CHUNKS):
         core[k].wait_send()
         rings[k].done()
@@ -532,7 +542,8 @@
     zring.done()
     for m in zys + [back]:
         m.done()
-    for cp in (first_all, second_all, third_all):
+    wt_last.wait()
+    for cp in (wt_swap, first_all, second_all, third_all):
         cp.wait_send()
 
 
@@ -561,9 +572,10 @@
             buf(2, 4, half_w, 8, chans),
             buf(2, CHUNKS, span * 8, chans),
             buf(2, 2, rows * 4, chans),
-            buf(*wt.shape),
             buf(8, *wt.shape[1:]),
-            dma(3), dma(CHUNKS, 2), dma(2), dma(2), dma(2),
+            buf(8, *wt.shape[1:]),
+            buf(8, *wt.shape[1:]),
+            dma(3), dma(CHUNKS, 2), dma(2), dma(2), dma(2), dma(2), dma(2),
             *coded_buffers(6 * CHUNKS, 2, span * 4, chans),
             *coded_buffers(CHUNKS, 1, span * 8, chans),
             *coded_buffers(6, 2, rows * 4, chans),

time: 87.9 us -> 86.8 us (0.987)
  Pallas kernels: 86.3 us -> 85.3 us
    pallas_call x1, Pallas kernels: 30 us -> 28.9 us  [reduce_all(): pl.pallas_call(reduce_kernel, out_shape=(jax.ShapeDtypeStruct((half_w, 8,...]
where the time goes in v8:
time: 86.8 us; the launch traced here: 86.6 us
  Pallas kernels  85.3 us (98%)
  between operations  1.3 us (1%)
    pallas_call x1, Pallas kernels, decode_runs(): pl.pallas_call(decode_kernel, out_shape=(jax.ShapeDtypeStruct((2 * labels...  33.1 us
    pallas_call x1, Pallas kernels, reduce_all(): pl.pallas_call(reduce_kernel, out_shape=(jax.ShapeDtypeStruct((half_w, 8,...  28.9 us
    pallas_call x1, Pallas kernels, exchange(): pl.pallas_call(exchange_kernel, out_shape=(jax.ShapeDtypeStruct(ids.shape...  19.5 us
    pallas_call x1, Pallas kernels, finish(): pl.pallas_call(finish_kernel, out_shape=(jax.ShapeDtypeStruct((hw_rows, c...  3.85 us

profile of v8, /device:TPU:0, one launch (start us, length us, event | category | flops | bytes accessed | tf_op | source)
XLA Modules:
  0.0 86.6 jit_solution(1891889173192690066)
XLA Ops:
  1.3 19.5 %shard_map.153 = (s32[1,512]{1,0:T(1,128)}, bf16[512,128]{1,0:T(8,128)(2,1)}, bf16[64,64,128]{2,1,0:T(8,128)(2,1)}, bf16[256,128]{1,0:T(8,128)(2,1)}) custom-call(s32[1,512]{1,0:T(1,128)} %ids_ref.5, s32[1,512]{1,0:T(1,128)} %ids_ref.5, bf16[4096,128]{1,0:T(8,128)(2,1)} %bitcast.16, bf16[64,32,128]{2,1,0:T(8,128)(2,1)} %zh_ref.1, s32[512,128]{1,0:T(8,128)} %bitcast.20), custom_call_target="tpu_custom_call" | custom-call | tf_op jit(solution)/shard_map/pallas_call | solution.py:102
  20.8 33.1 %shard_map.154 = (f32[1024,128]{1,0:T(8,128)}, f32[8,64,8,128]{3,2,1,0:T(8,128)}, f32[2,8,64,8,128]{4,3,2,1,0:T(8,128)}, f32[384,128]{1,0:T(8,128)}) custom-call(s32[1,512]{1,0:T(1,128)} %ids_ref.5, s32[1,512]{1,0:T(1,128)} %get-tuple-element.26.idx_ref, s32[1]{0:T(128)S(6)} %copy.17.count_ref, bf16[4096,128]{1,0:T(8,128)(2,1)} %bitcast.17, ...), custom_call_target="tpu_custom_call" | custom-call | tf_op jit(solution)/shard_map/pallas_call | solution.py:228
  53.8 28.9 %shard_map.155 = (f32[64,8,128]{2,1,0:T(8,128)}, f32[32,8,128]{2,1,0:T(8,128)}, f32[16,24,128]{2,1,0:T(8,128)}, f32[512,128]{1,0:T(8,128)}) custom-call(f32[2,2,4,64,8,128]{5,4,3,2,1,0:T(8,128)} %bitcast.15, f32[2,4,64,8,128]{4,3,2,1,0:T(8,128)} %bitcast.19, f32[16,24,128]{2,1,0:T(8,128)} %bitcast.22, f32[1024,128]{1,0:T(8,128)} %get-tuple-element.30.hw_hbm.own_ref), custom_call_target="tpu_custom_call" | custom-call | tf_op jit(solution)/shard_map/pallas_call | solution.py:558
  82.8 3.8 %shard_map.156 = (f32[4096,128]{1,0:T(8,128)}, f32[64,8,128]{2,1,0:T(8,128)}, f32[8,32,128]{2,1,0:T(8,128)}, f32[128,256]{1,0:T(8,128)}, f32[1,256]{1,0:T(1,128)}, /*index=5*/f32[18,256]{1,0:T(8,128)}, f32[1,18]{1,0:T(1,128)}) custom-call(s32[1,512]{1,0:T(1,128)} %ids_ref.5, s32[1]{0:T(128)S(6)} %copy.17.count_ref, ...), custom_call_target="tpu_custom_call" | custom-call | tf_op jit(solution)/shard_map/pallas_call | solution.py:292

commit v9 on v8

--- a/solution.py
+++ b/solution.py
@@ -12,7 +12,7 @@
 GRAD_SCALE = 0.25
 GROUP = 64
 CLS = 32
-CHUNKS = 2
+CHUNKS = 1
 EXCHANGE_VMEM = 58 * 1024 * 1024
 FINISH_VMEM = 58 * 1024 * 1024
 DECODE_VMEM = 58 * 1024 * 1024

time: 86.8 us -> 86.7 us (level)
  no operation moved by 1% of the time
where the time goes in v9:
time: 86.7 us; the launch traced here: 86.4 us
  Pallas kernels  85.1 us (98%)
  between operations  1.3 us (1%)
    pallas_call x1, Pallas kernels, decode_runs(): pl.pallas_call(decode_kernel, out_shape=(jax.ShapeDtypeStruct((2 * labels...  33 us
    pallas_call x1, Pallas kernels, reduce_all(): pl.pallas_call(reduce_kernel, out_shape=(jax.ShapeDtypeStruct((half_w, 8,...  28.7 us
    pallas_call x1, Pallas kernels, exchange(): pl.pallas_call(exchange_kernel, out_shape=(jax.ShapeDtypeStruct(ids.shape...  19.5 us
    pallas_call x1, Pallas kernels, finish(): pl.pallas_call(finish_kernel, out_shape=(jax.ShapeDtypeStruct((hw_rows, c...  3.85 us

profile of v9, /device:TPU:0, one launch (start us, length us, event | category | flops | bytes accessed | tf_op | source)
XLA Modules:
  0.0 86.4 jit_solution(14557276717374245346)
XLA Ops:
  1.3 19.5 %shard_map.153 = (s32[1,512]{1,0:T(1,128)}, bf16[512,128]{1,0:T(8,128)(2,1)}, bf16[64,64,128]{2,1,0:T(8,128)(2,1)}, bf16[256,128]{1,0:T(8,128)(2,1)}) custom-call(s32[1,512]{1,0:T(1,128)} %ids_ref.5, s32[1,512]{1,0:T(1,128)} %ids_ref.5, bf16[4096,128]{1,0:T(8,128)(2,1)} %bitcast.16, bf16[64,32,128]{2,1,0:T(8,128)(2,1)} %zh_ref.1, s32[512,128]{1,0:T(8,128)} %bitcast.20), custom_call_target="tpu_custom_call" | custom-call | tf_op jit(solution)/shard_map/pallas_call | solution.py:102
  20.8 33.0 %shard_map.154 = (f32[1024,128]{1,0:T(8,128)}, f32[8,64,8,128]{3,2,1,0:T(8,128)}, f32[2,8,64,8,128]{4,3,2,1,0:T(8,128)}, f32[384,128]{1,0:T(8,128)}) custom-call(s32[1,512]{1,0:T(1,128)} %ids_ref.5, s32[1,512]{1,0:T(1,128)} %get-tuple-element.26.idx_ref, s32[1]{0:T(128)S(6)} %copy.17.count_ref, bf16[4096,128]{1,0:T(8,128)(2,1)} %bitcast.17, ...), custom_call_target="tpu_custom_call" | custom-call | tf_op jit(solution)/shard_map/pallas_call | solution.py:228
  53.8 28.7 %shard_map.155 = (f32[64,8,128]{2,1,0:T(8,128)}, f32[32,8,128]{2,1,0:T(8,128)}, f32[16,24,128]{2,1,0:T(8,128)}, f32[512,128]{1,0:T(8,128)}) custom-call(f32[2,2,4,64,8,128]{5,4,3,2,1,0:T(8,128)} %bitcast.15, f32[2,4,64,8,128]{4,3,2,1,0:T(8,128)} %bitcast.19, f32[16,24,128]{2,1,0:T(8,128)} %bitcast.22, f32[1024,128]{1,0:T(8,128)} %get-tuple-element.30.hw_hbm.own_ref), custom_call_target="tpu_custom_call" | custom-call | tf_op jit(solution)/shard_map/pallas_call | solution.py:558
  82.5 3.8 %shard_map.156 = (f32[4096,128]{1,0:T(8,128)}, f32[64,8,128]{2,1,0:T(8,128)}, f32[8,32,128]{2,1,0:T(8,128)}, f32[128,256]{1,0:T(8,128)}, f32[1,256]{1,0:T(1,128)}, /*index=5*/f32[18,256]{1,0:T(8,128)}, f32[1,18]{1,0:T(1,128)}) custom-call(s32[1,512]{1,0:T(1,128)} %ids_ref.5, s32[1]{0:T(128)S(6)} %copy.17.count_ref, ...), custom_call_target="tpu_custom_call" | custom-call | tf_op jit(solution)/shard_map/pallas_call | solution.py:292
